TPU v7x, 128 devices: a whole 4x4x4 slice. The times are simulated.
128 devices in a mesh: dp: 16 (over y_lo, z, core), feat: 8 (over x, y_hi).
Axes of the slice: x: 4, y: 4 (y_hi: 2, y_lo: 2; y = y_hi * 2 + y_lo), z: 4, core: 2. Of those that a mesh axis runs over, the one named last changes fastest.
Arguments:
- emb_a: bfloat16 [2048, 1536], P('dp'), may hold values from -6 to 6
- emb_b: bfloat16 [2048, 1536], P('dp'), may hold values from -6 to 6
- w_in: bfloat16 [1536, 8192], P(None, 'feat'), may hold values from -0.15625 to 0.15625
- w_out: bfloat16 [8192, 8192], P(None, 'feat'), may hold values from -0.0625 to 0.0625
- gain: float32 [8192], P('feat'), may hold values from 0.5 to 1.5
- shift: float32 [8192], P('feat'), may hold values from -3 to 3
Outputs:
- grad_in: float32 [1536, 8192], P('dp', 'feat')
- grad_gain: float32 [8192], P('feat')
- grad_shift: float32 [8192], P('feat')
- diag_loss: float32 [8192], P('feat')
- row_loss: float32 [2048], P('dp')
All inputs are finite; a program needn't handle non-finite values.
Results may differ from a plain program's by a relative error of at most 0.019.
Values may be sent and summed in bfloat16 or wider, within the bound.
A program may use at most 128 MiB of HBM per device.

v0:
```python
import jax
import jax.numpy as jnp
from jax import lax
from jax.sharding import PartitionSpec as P

epsilon = 1e-05
off_weight = 0.0051


def moments(values, batch):
    center = lax.psum(jnp.sum(values, axis=1), "dp") / batch
    spread = lax.psum(jnp.sum((values - center[:, None, :]) ** 2, axis=1), "dp") / batch
    return (center[:, None, :], lax.rsqrt(spread + epsilon)[:, None, :])


def shards(emb_a, emb_b, w_in, w_out, gain, shift):
    local_rows = emb_a.shape[0]
    batch = local_rows * lax.axis_size("dp")
    width = w_out.shape[0]
    columns = w_out.shape[1]
    stacked = jnp.concatenate([emb_a, emb_b], axis=0)
    hidden = jnp.dot(stacked, w_in, preferred_element_type=jnp.float32).reshape(
        2, local_rows, columns
    )
    center, inverse = moments(hidden, batch)
    first_hat = (hidden - center) * inverse
    before = gain * first_hat + shift
    active = jnp.maximum(before, 0.0).astype(jnp.bfloat16).reshape(2 * local_rows, columns)
    block = w_out
    output = jnp.dot(
        lax.all_gather(active, "feat", axis=1, tiled=True),
        block,
        preferred_element_type=jnp.float32,
    ).reshape(2, local_rows, columns)
    center_out, inverse_out = moments(output, batch)
    second_hat = (output - center_out) * inverse_out
    normed = second_hat.astype(jnp.bfloat16)
    all_a, all_b = (
        lax.all_gather(normed[0], "dp", axis=0, tiled=True),
        lax.all_gather(normed[1], "dp", axis=0, tiled=True),
    )
    contract = (((1,), (1,)), ((), ()))
    part_a = lax.dot_general(normed[0], all_a, contract, preferred_element_type=jnp.float32)
    part_b = lax.dot_general(normed[1], all_b, contract, preferred_element_type=jnp.float32)
    gram_a, gram_b = (
        lax.psum(part_a.astype(jnp.bfloat16), "feat").astype(jnp.float32),
        lax.psum(part_b.astype(jnp.bfloat16), "feat").astype(jnp.float32),
    )
    corr_diag = jnp.sum(all_a.astype(jnp.float32) * all_b.astype(jnp.float32), axis=0) / batch
    diag_loss = (1.0 - corr_diag) ** 2 - off_weight * corr_diag**2
    row_loss = jnp.sum(gram_a * gram_b, axis=1) / (batch * width)
    factor = batch / 64.0
    column = -2.0 * (1.0 - corr_diag) - 2.0 * off_weight * corr_diag
    coeff = 2.0 * off_weight / (batch * batch)
    grad_norm_a = factor * (
        coeff * jnp.dot(gram_b.astype(jnp.bfloat16), all_a, preferred_element_type=jnp.float32)
        + normed[1].astype(jnp.float32) * column / batch
    )
    grad_norm_b = factor * (
        coeff * jnp.dot(gram_a.astype(jnp.bfloat16), all_b, preferred_element_type=jnp.float32)
        + normed[0].astype(jnp.float32) * column / batch
    )
    grad_norm = jnp.stack([grad_norm_a, grad_norm_b])
    sum_up, sum_dot = lax.psum(
        (jnp.sum(grad_norm, axis=1), jnp.sum(grad_norm * second_hat, axis=1)), "dp"
    )
    grad_out = inverse_out * (
        grad_norm - sum_up[:, None, :] / batch - second_hat * (sum_dot[:, None, :] / batch)
    )
    grad_out = grad_out.astype(jnp.bfloat16).reshape(2 * local_rows, columns)
    block = w_out
    grad_act = lax.psum_scatter(
        lax.dot_general(block, grad_out, contract, preferred_element_type=jnp.float32),
        "feat",
        scatter_dimension=0,
        tiled=True,
    ).T.reshape(2, local_rows, columns)
    grad_pre = jnp.where(before > 0, grad_act, 0.0)
    shift_sums, gain_sums = lax.psum(
        (jnp.sum(grad_pre, axis=1), jnp.sum(grad_pre * first_hat, axis=1)), "dp"
    )
    grad_hid = gain * (
        inverse
        * (grad_pre - shift_sums[:, None, :] / batch - first_hat * (gain_sums[:, None, :] / batch))
    )
    grad_hid = grad_hid.astype(jnp.bfloat16).reshape(2 * local_rows, columns)
    row_contract = (((0,), (0,)), ((), ()))
    grad_in = lax.psum_scatter(
        lax.dot_general(stacked, grad_hid, row_contract, preferred_element_type=jnp.float32),
        "dp",
        scatter_dimension=0,
        tiled=True,
    )
    return (
        grad_in,
        gain_sums[0] + gain_sums[1],
        shift_sums[0] + shift_sums[1],
        diag_loss,
        row_loss,
    )


def solution(mesh):
    return jax.shard_map(
        shards,
        mesh=mesh,
        in_specs=(
            P("dp", None),
            P("dp", None),
            P(None, "feat"),
            P(None, "feat"),
            P("feat"),
            P("feat"),
        ),
        out_specs=(P("dp", "feat"), P("feat"), P("feat"), P("feat"), P("dp")),
        check_vma=False,
    )
```

profile of v0, /device:TPU:0, one launch (start us, length us, event | category | flops | bytes accessed | tf_op | source)
XLA Modules:
  0.0 711.3 jit_solution(6048883790272965368)
XLA Ops:
  7.2 0.0 copy-start
  7.2 0.0 copy-start.9
  7.2 0.0 copy-start.10
  7.2 0.0 all-gather.6.cloned.1.call-start
  7.2 1.2 constant_dynamic-update-slice_fusion.1
  8.4 1.0 constant_dynamic-update-slice_fusion
  9.5 0.0 copy-start.7
  9.5 0.9 copy-done.7
  10.3 0.0 copy-done
  10.3 2.1 bitcast_reduce_fusion.1
  12.4 32.2 %psum.70 = f32[2,1024]{1,0:T(2,128)S(1)} all-reduce(f32[2,1024]{1,0:T(2,128)S(1)} %get-tuple-element.19), channel_id=1, replica_groups=mesh['dp'=16,'feat'=8] {'dp'}, use_global_device_ids=true, to_apply=%region_1.0 | all-reduce | flops 2048 | bytes 16384 | tf_op jit(solution)/shard_map/psum | solution.py:11
  44.6 1.4 multiply_reduce_fusion.5
  46.0 27.6 %psum.71 = f32[2,1024]{1,0:T(2,128)S(1)} all-reduce(f32[2,1024]{1,0:T(2,128)S(1)} %multiply_reduce_fusion.5), channel_id=1, replica_groups=mesh['dp'=16,'feat'=8] {'dp'}, use_global_device_ids=true, to_apply=%region_3.0 | all-reduce | flops 2048 | bytes 16384 | tf_op jit(solution)/shard_map/psum | solution.py:12
  73.6 0.0 copy-done.9
  73.7 0.0 copy-done.10
  73.7 2.2 maximum_convert_fusion
  75.9 0.0 all-gather.6.cloned.1.call-update
  75.9 0.0 all-gather.10.cloned.1.call-start
  76.0 70.2 %all-gather.6.cloned.1.call-done = bf16[256,8192]{1,0:T(8,128)(2,1)} async-done(((bf16[256,1024]{1,0:T(8,128)(2,1)}), bf16[256,8192]{1,0:T(8,128)(2,1)}) %all-gather.6.cloned.1.call-update) | async-done | bytes 4194320 | tf_op jit(solution)/shard_map/all_gather | solution.py:31
  146.1 12.5 %bitcast_reduce_fusion = (f32[2,1024]{1,0:T(2,128)S(1)}, f32[256,1024]{1,0:T(8,128)}) fusion(bf16[256,8192]{1,0:T(8,128)(2,1)} %all-gather.6.cloned.1.call-done, bf16[8192,1024]{1,0:T(8,128)(2,1)} %param.9), kind=kOutput, calls=%fused_computation.36 | convolution fusion | flops 4295227392 | bytes 22028288 | tf_op jit(solution)/shard_map/dot_general | solution.py:30
  158.7 29.6 %psum.72 = f32[2,1024]{1,0:T(2,128)S(1)} all-reduce(f32[2,1024]{1,0:T(2,128)S(1)} %get-tuple-element.21), channel_id=1, replica_groups=mesh['dp'=16,'feat'=8] {'dp'}, use_global_device_ids=true, to_apply=%region_5.0 | all-reduce | flops 2048 | bytes 16384 | tf_op jit(solution)/shard_map/psum | solution.py:11
  188.3 1.4 multiply_reduce_fusion.4
  189.7 27.6 %psum.73 = f32[2,1024]{1,0:T(2,128)S(1)} all-reduce(f32[2,1024]{1,0:T(2,128)S(1)} %multiply_reduce_fusion.4), channel_id=1, replica_groups=mesh['dp'=16,'feat'=8] {'dp'}, use_global_device_ids=true, to_apply=%region_7.0 | all-reduce | flops 2048 | bytes 16384 | tf_op jit(solution)/shard_map/psum | solution.py:12
  217.3 1.3 fusion.47
  218.7 0.0 copy-start.3
  218.7 0.8 copy-done.3
  219.5 0.8 fusion.55
  220.3 0.0 all-gather.10.cloned.1.call-update
  220.3 0.0 all-gather.8.cloned.1.call-start
  220.4 0.7 all-gather.8.cloned.1.call-update
  221.1 0.0 all-reduce.5.cloned.1.call-start
  221.1 33.0 %all-gather.10.cloned.1.call-done = bf16[1,2048,1024]{2,1,0:T(8,128)(2,1)} async-done(((bf16[1,128,1024]{2,1,0:T(8,128)(2,1)}), bf16[1,2048,1024]{2,1,0:T(8,128)(2,1)}) %all-gather.10.cloned.1.call-update) | async-done | bytes 4194320 | tf_op jit(solution)/shard_map/all_gather | solution.py:39
  254.2 4.6 fusion.11
  258.8 35.1 %all-gather.8.cloned.1.call-done = bf16[1,2048,1024]{2,1,0:T(8,128)(2,1)} async-done(((bf16[1,128,1024]{2,1,0:T(8,128)(2,1)}), bf16[1,2048,1024]{2,1,0:T(8,128)(2,1)}) %all-gather.8.cloned.1.call-update) | async-done | bytes 4194320 | tf_op jit(solution)/shard_map/all_gather | solution.py:40
  293.9 4.6 fusion.8
  298.5 0.0 all-reduce.5.cloned.1.call-update
  298.5 0.0 reduce-scatter.3.cloned.1.call-start
  298.6 5.1 multiply_reduce_fusion
  303.6 0.6 multiply_subtract_fusion
  304.2 83.3 %all-reduce.5.cloned.1.call-done = (bf16[128,2048]{1,0:T(8,128)(2,1)}, bf16[128,2048]{1,0:T(8,128)(2,1)}) async-done(((bf16[128,2048]{1,0:T(8,128)(2,1)}, bf16[128,2048]{1,0:T(8,128)(2,1)}), (bf16[128,2048]{1,0:T(8,128)(2,1)}, bf16[128,2048]{1,0:T(8,128)(2,1)})) %all-reduce.5.cloned.1.call-update) | async-done | bytes 1048592 | tf_op jit(solution)/shard_map/psum | solution.py:46
  387.6 3.3 fusion.35
  390.9 0.4 copy-done.1
  391.2 0.1 copy-done.4
  391.3 0.2 copy-done.8
  391.5 0.8 fusion.26
  392.3 0.3 multiply_reduce_fusion.3
  392.6 0.5 copy-done.6
  393.1 53.1 %all-reduce.1 = (f32[2,1024]{1,0:T(2,128)S(1)}, f32[2,1024]{1,0:T(2,128)S(1)}) all-reduce(f32[2,1024]{1,0:T(2,128)S(1)} %get-tuple-element.8, f32[2,1024]{1,0:T(2,128)S(1)} %get-tuple-element.7), channel_id=1, replica_groups=mesh['dp'=16,'feat'=8] {'dp'}, use_global_device_ids=true, to_apply=%region_12.0 | all-reduce | flops 4096 | bytes 32768 | tf_op jit(solution)/shard_map/psum | solution.py:64
  446.2 1.3 fusion.49
  447.5 2.2 fusion.42
  449.8 13.7 %convolution_bitcast_fusion = f32[8192,256]{0,1:T(8,128)} fusion(bf16[256,1024]{1,0:T(8,128)(2,1)} %fusion.42, bf16[8192,1024]{1,0:T(8,128)(2,1)} %param.9), kind=kOutput, calls=%fused_computation | convolution fusion | flops 4294967296 | bytes 25690112 | tf_op jit(solution)/shard_map/dot_general | solution.py:73
  463.5 0.0 reduce-scatter.3.cloned.1.call-update
  463.5 0.0 reduce-scatter.5.cloned.1.call-start
  463.6 110.3 %reduce-scatter.3.cloned.1.call-done = f32[1024,256]{0,1:T(8,128)} async-done(((f32[8192,256]{0,1:T(8,128)}), f32[1024,256]{0,1:T(8,128)}) %reduce-scatter.3.cloned.1.call-update) | async-done | bytes 1048592 | tf_op jit(solution)/shard_map/reduce_scatter | solution.py:72
  573.9 1.9 fusion.48
  575.8 54.6 %all-reduce = (f32[2,1024]{1,0:T(2,128)S(1)}, f32[2,1024]{1,0:T(2,128)S(1)}) all-reduce(f32[2,1024]{1,0:T(2,128)S(1)} %get-tuple-element.6, f32[2,1024]{1,0:T(2,128)S(1)} %get-tuple-element.5), channel_id=1, replica_groups=mesh['dp'=16,'feat'=8] {'dp'}, use_global_device_ids=true, to_apply=%region_19.20 | all-reduce | flops 4096 | bytes 32768 | tf_op jit(solution)/shard_map/psum | solution.py:79
  630.4 1.9 fusion.39
  632.3 4.8 fusion.56
  637.1 0.0 reduce-scatter.5.cloned.1.call-update
  637.2 1.4 multiply_reduce_fusion.1
  638.6 0.5 broadcast_multiply_fusion.6
  639.1 0.6 slice_add_fusion.1
  639.7 0.6 slice_add_fusion
  640.3 64.2 %reduce-scatter.5.cloned.1.call-done = f32[96,1024]{1,0:T(8,128)} async-done(((f32[1536,1024]{1,0:T(8,128)}), f32[96,1024]{1,0:T(8,128)}) %reduce-scatter.5.cloned.1.call-update) | async-done | bytes 393232 | tf_op jit(solution)/shard_map/reduce_scatter | solution.py:88
  (15 shorter events, 0.1 us)
Async XLA Ops:
  7.2 3.2 copy-start
  7.2 66.5 %copy-start.9 = (f32[1024]{0:T(1024)S(1)}, f32[1024]{0:T(1024)}, u32[]{:S(2)}) copy-start(f32[1024]{0:T(1024)} %param.11) | copy-start | bytes 12292
  7.2 66.5 %copy-start.10 = (f32[1024]{0:T(1024)S(1)}, f32[1024]{0:T(1024)}, u32[]{:S(2)}) copy-start(f32[1024]{0:T(1024)} %param.10) | copy-start | bytes 12292
  7.2 138.9 %all-gather.6.cloned.1.call-start = ((), (), s32[]{:S(2)}) async-start(), calls=%async_computation.2 | async-start | bytes 4718592 | tf_op jit(solution)/shard_map/all_gather | solution.py:31
  9.5 0.9 copy-start.7
  75.9 178.2 %all-gather.10.cloned.1.call-start = ((), (), s32[]{:S(2)}) async-start(), calls=%async_computation.6 | async-start | bytes 4456448 | tf_op jit(solution)/shard_map/all_gather | solution.py:39
  218.7 0.8 copy-start.3
  220.3 73.6 %all-gather.8.cloned.1.call-start = ((), (), s32[]{:S(2)}) async-start(), calls=%async_computation.5 | async-start | bytes 4456448 | tf_op jit(solution)/shard_map/all_gather | solution.py:40
  221.1 166.5 %all-reduce.5.cloned.1.call-start = ((), (), s32[]{:S(2)}) async-start(), calls=%async_computation.7 | async-start | bytes 2097152 | tf_op jit(solution)/shard_map/psum | solution.py:46
  298.5 275.4 %reduce-scatter.3.cloned.1.call-start = ((), (), s32[]{:S(2)}) async-start(), calls=%async_computation.3 | async-start | bytes 9437184 | tf_op jit(solution)/shard_map/reduce_scatter | solution.py:72
  387.5 3.7 copy-start.1
  387.6 3.8 copy-start.4
  387.6 4.0 copy-start.8
  387.6 4.8 copy-start.2
  390.9 1.8 copy-start.5
  392.3 0.8 copy-start.6
  463.5 241.0 %reduce-scatter.5.cloned.1.call-start = ((), (), s32[]{:S(2)}) async-start(), calls=%async_computation.4 | async-start | bytes 6684672 | tf_op jit(solution)/shard_map/reduce_scatter | solution.py:88
Sparse Core Ops, SparseCore 0:
  76.0 70.0 all-gather.5
  220.5 33.6 all-gather.9
  256.4 37.4 all-gather.7
  298.6 88.8 all-reduce.4
  463.6 110.2 reduce-scatter.2
  637.3 67.1 reduce-scatter.4
where the time goes:
time: 712 us; the launch traced here: 711 us
  waiting for transfers between devices  397 us (56%)
  blocking collectives  225 us (32%)
  matrix products  46.4 us (7%)
  other arithmetic  22.8 us (3%)
  between operations  14.3 us (2%)
    reduce_scatter x1, waiting for transfers between devices, shards(): lax.psum_scatter(lax.dot_general(block, grad_out, contract, preferred_ele...  110 us
    psum x1, waiting for transfers between devices, shards(): lax.psum(part_a.astype(jnp.bfloat16), 'feat').astype(jnp.float32)  83.3 us
    all_gather x1, waiting for transfers between devices, shards(): lax.all_gather(active, 'feat', axis=1, tiled=True)  70.2 us
    reduce_scatter x1, waiting for transfers between devices, shards(): lax.psum_scatter(lax.dot_general(stacked, grad_hid, row_contract, preferr...  64.2 us
    psum x2, blocking collectives, moments(): center = lax.psum(jnp.sum(values, axis=1), 'dp') / batch  61.8 us
    psum x2, blocking collectives, moments(): lax.psum(jnp.sum((values - center[:, None, :]) ** 2, axis=1), 'dp') / batch  55.3 us
    psum x1, blocking collectives, shards(): lax.psum((jnp.sum(grad_pre, axis=1), jnp.sum(grad_pre * first_hat, axis=1...  54.6 us
    psum x1, blocking collectives, shards(): lax.psum((jnp.sum(grad_norm, axis=1), jnp.sum(grad_norm * second_hat, axi...  53.1 us
  transfers between devices with their start and end apart: 6, of which 6 were waited for; matrix products, arithmetic and copies ran while one was open for 2% of the time, Pallas kernels for 0%

commit v1 on v0

v1 whole, which is shorter than its diff:
```python
import functools

import jax
import jax.numpy as jnp
from jax import lax
from jax.experimental import pallas as pl
from jax.experimental.pallas import tpu as pltpu
from jax.sharding import PartitionSpec as P

MESH = pl.DeviceIdType.MESH
epsilon = 1e-05
off_weight = 0.0051
BATCH = 2048
ROWS = 128
WIDE = 1024
EMB = 1536
DP = 16
FEAT = 8
OUT = EMB // DP
TILE = 256
HALF = ROWS // 2
f32 = jnp.float32
bf16 = jnp.bfloat16
NT = (((1,), (1,)), ((), ()))


def column_tiles(body, width=WIDE, tile=TILE):
    @pl.loop(0, width // tile)
    def _(i):
        body(pl.ds(pl.multiple_of(i * tile, tile), tile))


def kernel(
    emb_a, emb_b, w_in, w_out, gain, shift,
    grad_in, grad_gain, grad_shift, diag_loss, row_loss,
    emb, win, wout, gn_sh, inv, hid, act, out, st1, st2, st3, st4, nrm, corr,
    part, far_g, near_gs, near_gr, y_gs, y_gr, gram, go,
    far_s, far_r, near_s, near_r, ys, yr, gact, gh, emb_t,
    core_s, core_r, own_p, far_is, far_ir, near_is, near_ir, y_is, y_ir, gout,
    send_sem, recv_sem, local_sem,
):
    dp, ft = lax.axis_index("dp"), lax.axis_index("feat")
    core, z = lax.rem(dp, 2), lax.rem(dp // 2, 4)
    y_lo, x, y_hi = dp // 8, ft // 2, lax.rem(ft, 2)

    def at_x(step):
        return lax.rem(x + step + 4, 4)

    def at_z(step):
        return lax.rem(z + step + 4, 4)

    def feat_of(step, flip=0):
        return at_x(step) * 2 + (y_hi + flip * (1 - 2 * y_hi))

    def dp_of(step, flip_y=0, flip_core=0):
        yy = y_lo + flip_y * (1 - 2 * y_lo)
        return (yy * 4 + at_z(step)) * 2 + (core + flip_core * (1 - 2 * core))

    x_right, x_left, y_pair = (dp, feat_of(1)), (dp, feat_of(-1)), (dp, feat_of(0, 1))
    z_right, z_left = (dp_of(1), ft), (dp_of(-1), ft)
    y_next, other = (dp_of(0, 1), ft), (dp_of(0, 0, 1), ft)
    peers = [(lax.rem(dp + k, DP), ft) for k in range(1, DP)]

    started = []
    counts = [0, 0]

    def send(src, dst, device):
        i = counts[0]
        counts[0] += 1
        copy = pltpu.make_async_remote_copy(
            src_ref=src, dst_ref=dst, send_sem=send_sem.at[i], recv_sem=recv_sem.at[i],
            device_id=device, device_id_type=MESH,
        )
        copy.start()
        started.append(copy)
        return copy

    def fetch(src, dst):
        i = counts[1]
        counts[1] += 1
        copy = pltpu.make_async_copy(src, dst, local_sem.at[i])
        copy.start()
        return copy

    in_emb = [fetch(emb_a, emb.at[pl.ds(0, ROWS)]), fetch(emb_b, emb.at[pl.ds(ROWS, ROWS)])]
    in_win = fetch(w_in, win)
    in_gs = [fetch(gain, gn_sh.at[pl.ds(0, 1)]), fetch(shift, gn_sh.at[pl.ds(1, 1)])]
    in_wout = fetch(w_out, wout)

    barrier = pltpu.get_barrier_semaphore()
    greeted = peers + [x_right, x_left, y_pair]
    for device in greeted:
        pl.semaphore_signal(barrier, inc=1, device_id=device, device_id_type=MESH)

    def rows(v):
        return pl.ds(v * ROWS, ROWS)

    def share(table):
        return [send(table.at[dp], table.at[dp], device) for device in peers]

    def local_moments(values, table, v, cols):
        center = jnp.sum(values, axis=0, keepdims=True) / ROWS
        spread = jnp.sum((values - center) ** 2, axis=0, keepdims=True)
        table[dp, 0:1, cols] = center
        table[dp, 1:2, cols] = spread

    def global_moments(table, cols):
        centers = table[:, 0, cols]
        center = jnp.sum(centers, axis=0, keepdims=True) / DP
        spread = jnp.sum(table[:, 1, cols], axis=0, keepdims=True) + ROWS * jnp.sum(
            (centers - center) ** 2, axis=0, keepdims=True
        )
        return center, lax.rsqrt(spread / BATCH + epsilon)

    def first_layer():
        for copy in in_emb:
            copy.wait()
        in_win.wait()

        def tile(cols):
            product = jnp.dot(emb[...], win[:, cols], preferred_element_type=f32)
            for v in range(2):
                piece = product[v * ROWS : (v + 1) * ROWS]
                hid[v, :, cols] = piece
                local_moments(piece, st1.at[v], v, cols)

        column_tiles(tile)
        pl.semaphore_wait(barrier, len(greeted))

    def first_norm(v):
        copies = share(st1.at[v])
        yield
        for copy in copies:
            copy.wait_recv()
        if v == 0:
            for copy in in_gs:
                copy.wait()

        def tile(cols):
            center, inverse = global_moments(st1.at[v], cols)
            hat = (hid[v, :, cols] - center) * inverse
            hid[v, :, cols] = hat
            inv[v : v + 1, cols] = inverse
            before = gn_sh[0:1, cols] * hat + gn_sh[1:2, cols]
            act[v, ft, :, cols] = jnp.maximum(before, 0.0).astype(bf16)

        column_tiles(tile)

    def project(v, slot, first=False):
        def tile(cols):
            product = jnp.dot(
                act[v, slot], wout[pl.ds(pl.multiple_of(slot * WIDE, WIDE), WIDE), cols],
                preferred_element_type=f32,
            )
            if first:
                out[v, :, cols] = product
            else:
                out[v, :, cols] += product

        column_tiles(tile)

    def gather_feat(v):
        low, high = pl.ds(0, HALF), pl.ds(HALF, HALF)
        mine, pair = ft, feat_of(0, 1)

        def go_(slot, device, part_rows=None):
            ref = act.at[v, slot] if part_rows is None else act.at[v, slot, part_rows]
            return send(ref, ref, device)

        a = go_(mine, y_pair)
        b = go_(mine, x_right)
        c = go_(mine, x_left)
        if v == 0:
            in_wout.wait()
        project(v, mine, first=True)
        yield
        a.wait_recv()
        d = go_(pair, x_right)
        e = go_(pair, x_left)
        project(v, pair)
        yield
        b.wait_recv()
        f = go_(feat_of(-1), x_right, low)
        c.wait_recv()
        g = go_(feat_of(1), x_left, high)
        project(v, feat_of(-1))
        project(v, feat_of(1))
        yield
        d.wait_recv()
        h = go_(feat_of(-1, 1), x_right, low)
        e.wait_recv()
        i = go_(feat_of(1, 1), x_left, high)
        project(v, feat_of(-1, 1))
        project(v, feat_of(1, 1))
        yield
        f.wait_recv()
        g.wait_recv()
        project(v, feat_of(2))
        yield
        h.wait_recv()
        i.wait_recv()
        project(v, feat_of(2, 1))

    def second_norm(v):
        column_tiles(lambda cols: local_moments(out[v, :, cols], st2.at[v], v, cols))
        copies = share(st2.at[v])
        yield
        for copy in copies:
            copy.wait_recv()

        def tile(cols):
            center, inverse = global_moments(st2.at[v], cols)
            hat = (out[v, :, cols] - center) * inverse
            out[v, :, cols] = hat
            inv[2 + v : 3 + v, cols] = inverse
            nrm[v, dp, :, cols] = hat.astype(bf16)

        column_tiles(tile)

    def inner(v, slot):
        cols = pl.ds(pl.multiple_of(slot * ROWS, ROWS), ROWS)
        part[v, :, cols] = lax.dot_general(
            nrm[v, dp], nrm[v, slot], NT, preferred_element_type=f32
        ).astype(bf16)
        if v == 1:
            corr[pl.ds(slot, 1), :] = jnp.sum(
                nrm[0, slot].astype(f32) * nrm[1, slot].astype(f32), axis=0, keepdims=True
            )

    def gather_dp(v):
        low, high = pl.ds(0, HALF), pl.ds(HALF, HALF)

        def go_(slot, device, part_rows=None):
            ref = nrm.at[v, slot] if part_rows is None else nrm.at[v, slot, part_rows]
            return send(ref, ref, device)

        cores = []

        def have(step, flip):
            slot = dp_of(step, flip)
            cores.append((go_(slot, other), step, flip))
            inner(v, slot)

        def from_core(count):
            for _ in range(count):
                copy, step, flip = cores.pop(0)
                copy.wait_recv()
                inner(v, dp_of(step, flip, 1))

        a = go_(dp, y_next)
        b = go_(dp, z_right)
        c = go_(dp, z_left)
        have(0, 0)
        yield
        a.wait_recv()
        d = go_(dp_of(0, 1), z_right)
        e = go_(dp_of(0, 1), z_left)
        have(0, 1)
        from_core(1)
        yield
        b.wait_recv()
        f = go_(dp_of(-1), z_right, low)
        c.wait_recv()
        g = go_(dp_of(1), z_left, high)
        have(-1, 0)
        have(1, 0)
        from_core(1)
        yield
        d.wait_recv()
        h = go_(dp_of(-1, 1), z_right, low)
        e.wait_recv()
        i = go_(dp_of(1, 1), z_left, high)
        have(-1, 1)
        have(1, 1)
        from_core(2)
        yield
        f.wait_recv()
        g.wait_recv()
        have(2, 0)
        from_core(2)
        yield
        h.wait_recv()
        i.wait_recv()
        have(2, 1)
        from_core(2)

    def sum_gram(v):
        low, high = pl.ds(0, BATCH // 2), pl.ds(BATCH // 2, BATCH // 2)

        def pair_rows(step):
            return pl.ds(pl.multiple_of(at_x(step) * 32, 32), 32)

        far_right = send(part.at[v, pair_rows(2), low], far_g.at[v, 0], x_right)
        far_left = send(part.at[v, pair_rows(2), high], far_g.at[v, 1], x_left)
        near_gs[v, 0] = part[v, pair_rows(1), :]
        near_gs[v, 1] = part[v, pair_rows(-1), :]
        near = [
            send(near_gs.at[v, 0, :, high], near_gr.at[v, 0, :, high], x_right),
            send(near_gs.at[v, 1, :, low], near_gr.at[v, 1, :, low], x_left),
        ]
        yield
        far_right.wait_recv()
        near_gs[v, 0, :, low] = (
            near_gs[v, 0, :, low].astype(f32) + far_g[v, 0].astype(f32)
        ).astype(bf16)
        near.append(send(near_gs.at[v, 0, :, low], near_gr.at[v, 0, :, low], x_right))
        far_left.wait_recv()
        near_gs[v, 1, :, high] = (
            near_gs[v, 1, :, high].astype(f32) + far_g[v, 1].astype(f32)
        ).astype(bf16)
        near.append(send(near_gs.at[v, 1, :, high], near_gr.at[v, 1, :, high], x_left))
        yield
        for copy in near:
            copy.wait_recv()

        def line_sum(flip):
            h = y_hi + flip * (1 - 2 * y_hi)
            block = pl.ds(pl.multiple_of(h * 16, 16), 16)
            return (
                part[v, pl.ds(pl.multiple_of(feat_of(0, flip) * 16, 16), 16), :].astype(f32)
                + near_gr[v, 0, block, :].astype(f32)
                + near_gr[v, 1, block, :].astype(f32)
            )

        y_gs[v] = line_sum(1).astype(bf16)
        a = send(y_gs.at[v], y_gr.at[v], y_pair)
        yield
        a.wait_recv()

        def slot(step, flip=0):
            return pl.ds(pl.multiple_of(feat_of(step, flip) * 16, 16), 16)

        gram[v, slot(0), :] = (line_sum(0) + y_gr[v].astype(f32)).astype(bf16)

        def go_(block, device, cols=None):
            ref = gram.at[v, block] if cols is None else gram.at[v, block, cols]
            return send(ref, ref, device)

        a = go_(slot(0), y_pair)
        b = go_(slot(0), x_right)
        c = go_(slot(0), x_left)
        yield
        a.wait_recv()
        d = go_(slot(0, 1), x_right)
        e = go_(slot(0, 1), x_left)
        b.wait_recv()
        f = go_(slot(-1), x_right, low)
        c.wait_recv()
        g = go_(slot(1), x_left, high)
        yield
        d.wait_recv()
        h = go_(slot(-1, 1), x_right, low)
        e.wait_recv()
        i = go_(slot(1, 1), x_left, high)
        yield
        for copy in (f, g, h, i):
            copy.wait_recv()

    factor = BATCH / 64.0
    coeff = 2.0 * off_weight / (BATCH * BATCH)

    def losses():
        diag = jnp.sum(corr[...], axis=0, keepdims=True) / BATCH
        diag_loss[...] = (1.0 - diag) ** 2 - off_weight * diag**2
        corr[0:1, :] = -2.0 * (1.0 - diag) - 2.0 * off_weight * diag

    def row_losses():
        total = jnp.zeros((ROWS, ROWS), f32)
        for k in range(BATCH // ROWS):
            cols = slice(k * ROWS, (k + 1) * ROWS)
            total += gram[0, :, cols].astype(f32) * gram[1, :, cols].astype(f32)
        total = jnp.sum(total.T, axis=0, keepdims=True)
        row_loss[...] = total / (BATCH * WIDE * FEAT)

    def output_back(v):
        def tile(cols):
            product = jnp.dot(
                gram[1 - v], nrm[v, :, :, cols].reshape(BATCH, TILE), preferred_element_type=f32
            )
            upstream = factor * (
                coeff * product + nrm[1 - v, dp, :, cols].astype(f32) * corr[0:1, cols] / BATCH
            )
            gact[v, :, cols] = upstream
            st3[v, dp, 0:1, cols] = jnp.sum(upstream, axis=0, keepdims=True)
            st3[v, dp, 1:2, cols] = jnp.sum(upstream * out[v, :, cols], axis=0, keepdims=True)

        column_tiles(tile)
        copies = share(st3.at[v])
        yield
        for copy in copies:
            copy.wait_recv()

        def finish(cols):
            up = jnp.sum(st3[v, :, 0, cols], axis=0, keepdims=True) / BATCH
            dot = jnp.sum(st3[v, :, 1, cols], axis=0, keepdims=True) / BATCH
            go[v, :, cols] = (
                inv[2 + v : 3 + v, cols] * (gact[v, :, cols] - up - out[v, :, cols] * dot)
            ).astype(bf16)

        column_tiles(finish)

    def active_back(v):
        def block(step, flip, store):
            first = feat_of(step, flip) * WIDE

            def tile(cols):
                store(
                    cols,
                    lax.dot_general(
                        go[v], wout[pl.ds(pl.multiple_of(first + cols.start, TILE), TILE), :], NT,
                        preferred_element_type=f32,
                    ),
                )

            column_tiles(tile)

        low, high = pl.ds(0, HALF), pl.ds(HALF, HALF)

        def keep(ref):
            def store(cols, value):
                ref[:, cols] = value.astype(bf16)

            return store

        def far(flip):
            block(2, flip, keep(far_s.at[v, flip]))
            return [
                send(far_s.at[v, flip, low], far_r.at[v, flip, 0], x_right),
                send(far_s.at[v, flip, high], far_r.at[v, flip, 1], x_left),
            ]

        def near(flip):
            block(1, flip, keep(near_s.at[v, flip, 0]))
            a = send(near_s.at[v, flip, 0, high], near_r.at[v, flip, 0, high], x_right)
            block(-1, flip, keep(near_s.at[v, flip, 1]))
            b = send(near_s.at[v, flip, 1, low], near_r.at[v, flip, 1, low], x_left)
            return [a, b]

        def relay(flip, fars, nears):
            for side, half, device in ((0, low, x_right), (1, high, x_left)):
                fars[side].wait_recv()
                near_s[v, flip, side, half] = (
                    near_s[v, flip, side, half].astype(f32) + far_r[v, flip, side].astype(f32)
                ).astype(bf16)
                nears.append(
                    send(near_s.at[v, flip, side, half], near_r.at[v, flip, side, half], device)
                )

        fars1 = far(1)
        nears1 = near(1)
        yield
        fars0 = far(0)
        relay(1, fars1, nears1)
        nears0 = near(0)
        yield

        def store_own(cols, value):
            gact[v, :, cols] = value

        block(0, 1, store_own)
        for copy in nears1:
            copy.wait_recv()
        ys[v] = (
            gact[v] + near_r[v, 1, 0].astype(f32) + near_r[v, 1, 1].astype(f32)
        ).astype(bf16)
        last = send(ys.at[v], yr.at[v], y_pair)
        yield
        relay(0, fars0, nears0)
        block(0, 0, store_own)
        yield
        for copy in nears0 + [last]:
            copy.wait_recv()

    def first_back(v):
        def tile(cols):
            hat = hid[v, :, cols]
            grad = (
                gact[v, :, cols]
                + near_r[v, 0, 0, :, cols].astype(f32)
                + near_r[v, 0, 1, :, cols].astype(f32)
                + yr[v, :, cols].astype(f32)
            )
            before = gn_sh[0:1, cols] * hat + gn_sh[1:2, cols]
            grad = jnp.where(before > 0, grad, 0.0)
            gact[v, :, cols] = grad
            st4[v, dp, 0:1, cols] = jnp.sum(grad, axis=0, keepdims=True)
            st4[v, dp, 1:2, cols] = jnp.sum(grad * hat, axis=0, keepdims=True)

        column_tiles(tile)
        copies = share(st4.at[v])
        yield
        for copy in copies:
            copy.wait_recv()

        def finish(cols):
            up = jnp.sum(st4[v, :, 0, cols], axis=0, keepdims=True)
            dot = jnp.sum(st4[v, :, 1, cols], axis=0, keepdims=True)
            gh[rows(v), cols] = (
                gn_sh[0:1, cols] * inv[v : v + 1, cols]
                * (gact[v, :, cols] - up / BATCH - hid[v, :, cols] * (dot / BATCH))
            ).astype(bf16)
            if v == 0:
                grad_shift[:, cols] = up
                grad_gain[:, cols] = dot
            else:
                grad_shift[:, cols] += up
                grad_gain[:, cols] += dot

        column_tiles(finish)

    def transpose_emb():
        for k in range(EMB // ROWS):
            cols = slice(k * ROWS, (k + 1) * ROWS)
            emb_t[cols, :] = emb[:, cols].T

    def last_layer():
        low, high = pl.ds(0, OUT // 2), pl.ds(OUT // 2, OUT // 2)

        def partial(step, flip_y, flip_core, store):
            target = dp_of(step, flip_y, flip_core)
            left = emb_t[pl.ds(pl.multiple_of(target * OUT, OUT), OUT), :]
            column_tiles(
                lambda cols: store(
                    cols, jnp.dot(left, gh[:, cols], preferred_element_type=f32)
                )
            )

        order = [(2, 1), (1, 1), (-1, 1), (2, 0), (1, 0), (-1, 0), (0, 1), (0, 0)]
        crossing = {}
        for n, (step, flip) in enumerate(order):
            def store(cols, value, n=n):
                core_s[n, :, cols] = value.astype(bf16)

            partial(step, flip, 1, store)
            crossing[step, flip] = send(core_s.at[n], core_r.at[n], other)

        def chip_sum(step, flip, keep):
            n = order.index((step, flip))

            def store(cols, value):
                own_p[n, :, cols] = value

            partial(step, flip, 0, store)
            crossing[step, flip].wait_recv()

            def tile(cols):
                keep(cols, own_p[n, :, cols] + core_r[n, :, cols].astype(f32))

            column_tiles(tile)

        def keep(ref):
            def store(cols, value):
                ref[:, cols] = value.astype(bf16)

            return store

        def far(flip):
            chip_sum(2, flip, keep(far_is.at[flip]))
            return [
                send(far_is.at[flip, low], far_ir.at[flip, 0], z_right),
                send(far_is.at[flip, high], far_ir.at[flip, 1], z_left),
            ]

        def near(flip):
            chip_sum(1, flip, keep(near_is.at[flip, 0]))
            a = send(near_is.at[flip, 0, high], near_ir.at[flip, 0, high], z_right)
            chip_sum(-1, flip, keep(near_is.at[flip, 1]))
            b = send(near_is.at[flip, 1, low], near_ir.at[flip, 1, low], z_left)
            return [a, b]

        def relay(flip, fars, nears):
            for side, half, device in ((0, low, z_right), (1, high, z_left)):
                fars[side].wait_recv()
                near_is[flip, side, half] = (
                    near_is[flip, side, half].astype(f32) + far_ir[flip, side].astype(f32)
                ).astype(bf16)
                nears.append(
                    send(near_is.at[flip, side, half], near_ir.at[flip, side, half], device)
                )

        def line_sum(flip, store):
            n = order.index((0, flip))

            def tile(cols):
                store(
                    cols,
                    own_p[n, :, cols]
                    + near_ir[flip, 0, :, cols].astype(f32)
                    + near_ir[flip, 1, :, cols].astype(f32),
                )

            column_tiles(tile)

        fars1 = far(1)
        nears1 = near(1)
        fars0 = far(0)
        relay(1, fars1, nears1)
        nears0 = near(0)

        def own(flip):
            n = order.index((0, flip))

            def store(cols, value):
                own_p[n, :, cols] = value

            chip_sum(0, flip, store)

        own(1)
        for copy in nears1:
            copy.wait_recv()
        line_sum(1, keep(y_is))
        last = send(y_is, y_ir, y_next)
        relay(0, fars0, nears0)
        own(0)
        for copy in nears0 + [last]:
            copy.wait_recv()

        def finish(cols, value):
            gout[:, cols] = value + y_ir[:, cols].astype(f32)

        line_sum(0, finish)
        store_out = fetch(gout, grad_in)
        store_out.wait()

    def together(*stages):
        stages = list(stages)
        while stages:
            for stage in list(stages):
                if next(stage, True):
                    stages.remove(stage)

    both = lambda stage: together(stage(0), stage(1))
    first_layer()
    both(first_norm)
    transpose_emb()
    both(gather_feat)
    both(second_norm)
    both(gather_dp)
    losses()
    both(sum_gram)
    both(output_back)
    row_losses()
    both(active_back)
    both(first_back)
    last_layer()
    for copy in started:
        copy.wait_send()


def scratch():
    v = pltpu.VMEM
    return [
        v((2 * ROWS, EMB), bf16), v((EMB, WIDE), bf16), v((FEAT * WIDE, WIDE), bf16),
        v((2, WIDE), f32), v((4, WIDE), f32), v((2, ROWS, WIDE), f32), v((2, FEAT, ROWS, WIDE), bf16),
        v((2, ROWS, WIDE), f32),
        v((2, DP, 2, WIDE), f32), v((2, DP, 2, WIDE), f32),
        v((2, DP, 2, WIDE), f32), v((2, DP, 2, WIDE), f32),
        v((2, DP, ROWS, WIDE), bf16), v((DP, WIDE), f32),
        v((2, ROWS, BATCH), bf16), v((2, 2, 32, BATCH // 2), bf16),
        v((2, 2, 32, BATCH), bf16), v((2, 2, 32, BATCH), bf16),
        v((2, 16, BATCH), bf16), v((2, 16, BATCH), bf16), v((2, ROWS, BATCH), bf16),
        v((2, ROWS, WIDE), bf16),
        v((2, 2, ROWS, WIDE), bf16), v((2, 2, 2, HALF, WIDE), bf16),
        v((2, 2, 2, ROWS, WIDE), bf16), v((2, 2, 2, ROWS, WIDE), bf16),
        v((2, ROWS, WIDE), bf16), v((2, ROWS, WIDE), bf16), v((2, ROWS, WIDE), f32),
        v((2 * ROWS, WIDE), bf16), v((EMB, 2 * ROWS), bf16),
        v((8, OUT, WIDE), bf16), v((8, OUT, WIDE), bf16), v((8, OUT, WIDE), f32),
        v((2, OUT, WIDE), bf16), v((2, 2, OUT // 2, WIDE), bf16),
        v((2, 2, OUT, WIDE), bf16), v((2, 2, OUT, WIDE), bf16),
        v((OUT, WIDE), bf16), v((OUT, WIDE), bf16), v((OUT, WIDE), f32),
        pltpu.SemaphoreType.DMA((260,)), pltpu.SemaphoreType.DMA((260,)),
        pltpu.SemaphoreType.DMA((8,)),
    ]


def shards(emb_a, emb_b, w_in, w_out, gain, shift):
    anywhere = pl.BlockSpec(memory_space=pl.ANY)
    near = pl.BlockSpec(memory_space=pltpu.VMEM)
    results = pl.pallas_call(
        kernel,
        out_shape=(
            jax.ShapeDtypeStruct((OUT, WIDE), f32),
            jax.ShapeDtypeStruct((1, WIDE), f32),
            jax.ShapeDtypeStruct((1, WIDE), f32),
            jax.ShapeDtypeStruct((1, WIDE), f32),
            jax.ShapeDtypeStruct((1, ROWS), f32),
        ),
        in_specs=[anywhere] * 6,
        out_specs=(anywhere, near, near, near, near),
        scratch_shapes=scratch(),
        compiler_params=pltpu.CompilerParams(
            collective_id=0, has_side_effects=True, vmem_limit_bytes=62 * 2**20
        ),
        cost_estimate=pl.CostEstimate(flops=14 * 10**9, bytes_accessed=24 * 2**20, transcendentals=0),
    )(emb_a, emb_b, w_in, w_out, gain.reshape(1, WIDE), shift.reshape(1, WIDE))
    return (results[0],) + tuple(r.reshape(-1) for r in results[1:])


def solution(mesh):
    return jax.shard_map(
        shards,
        mesh=mesh,
        in_specs=(
            P("dp", None), P("dp", None), P(None, "feat"), P(None, "feat"), P("feat"), P("feat"),
        ),
        out_specs=(P("dp", "feat"), P("feat"), P("feat"), P("feat"), P("dp")),
        check_vma=False,
    )
```

time: 712 us -> 211 us (0.30)
  waiting for transfers between devices: 397 us -> 0 us
  blocking collectives: 225 us -> 0 us
  Pallas kernels: 0 us -> 203 us
  matrix products: 46.4 us -> 0 us
  other arithmetic: 22.8 us -> 0 us
  between operations: 14.3 us -> 0.64 us
    psum x6 -> x0, blocking collectives: 225 us -> none  [the longest x2 61.8 us: moments(): center = lax.psum(jnp.sum(values, axis=1), 'dp') / batch]
    pallas_call x0 -> x1, Pallas kernels: none -> 203 us  [shards(): pl.pallas_call(kernel, out_shape=(jax.ShapeDtypeStruct((OUT, WIDE), f32),...]
    reduce_scatter x2 -> x0, waiting for transfers between devices: 175 us -> none  [the longest x1 110 us: shards(): lax.psum_scatter(lax.dot_general(block, grad_out, contract, preferred_ele...]
    all_gather x3 -> x0, waiting for transfers between devices: 138 us -> none  [the longest x1 70.2 us: shards(): lax.all_gather(active, 'feat', axis=1, tiled=True)]
    psum x1 -> x0, waiting for transfers between devices: 83.3 us -> none  [shards(): lax.psum(part_a.astype(jnp.bfloat16), 'feat').astype(jnp.float32)]
    dot_general x8 -> x0, matrix products: 46.4 us -> none  [the longest x1 13.7 us: shards(): lax.dot_general(block, grad_out, contract, preferred_element_type=jnp.flo...]
    reduce_sum x6 -> x0, other arithmetic: 11.4 us -> none  [the longest x1 5.06 us: shards(): jnp.sum(all_a.astype(jnp.float32) * all_b.astype(jnp.float32), axis=0)]
    convert_element_type x4 -> x0, other arithmetic: 7.74 us -> none  [the longest x1 2.24 us: shards(): grad_out = grad_out.astype(jnp.bfloat16).reshape(2 * local_rows, columns)]
  transfers between devices with their start and end apart: 6 -> 0, of which waited for: 6 -> 0; matrix products, arithmetic and copies ran while one was open for 2% -> 0% of each run, Pallas kernels for 0% -> 0%
where the time goes in v1:
time: 211 us
  Pallas kernels  203 us (96%)
  local copies, waits for them, and re-layouts  6.75 us (3%)
    pallas_call x1, Pallas kernels, shards(): pl.pallas_call(kernel, out_shape=(jax.ShapeDtypeStruct((OUT, WIDE), f32),...  203 us
    unnamed x5, local copies, waits for them, and re-layouts  6.75 us

profile of v1, /device:TPU:0, one launch (start us, length us, event | category | flops | bytes accessed | tf_op | source)
XLA Modules:
  0.0 210.7 jit_solution(3731217800926974310)
XLA Ops:
  0.6 203.3 %shard_map.101 = (f32[96,1024]{1,0:T(8,128)}, f32[1,1024]{1,0:T(1,128)}, f32[1,1024]{1,0:T(1,128)}, f32[1,1024]{1,0:T(1,128)}, f32[1,128]{1,0:T(1,128)}) custom-call(bf16[128,1536]{1,0:T(8,128)(2,1)} %emb_a.1, bf16[128,1536]{1,0:T(8,128)(2,1)} %emb_b.1, bf16[1536,1024]{1,0:T(8,128)(2,1)} %w_in.1, bf16[8192,1024]{1,0:T(8,128)(2,1)} %w_out.1, ...), custom_call_target="tpu_custom_call" | custom-call | flops 14000000000 | bytes 25165824 | tf_op jit(solution)/shard_map/pallas_call | solution.py:679
  204.0 1.8 copy.16
  205.7 1.3 copy.17
  207.0 1.3 copy.18
  208.3 1.3 copy.19
  209.5 1.2 copy.20

commit v2 on v1

--- a/solution.py
+++ b/solution.py
@@ -1,4 +1,5 @@
 import functools
+import math
 
 import jax
 import jax.numpy as jnp
@@ -18,6 +19,7 @@
 FEAT = 8
 OUT = EMB // DP
 TILE = 256
+PIECE = WIDE // 2
 HALF = ROWS // 2
 f32 = jnp.float32
 bf16 = jnp.bfloat16
@@ -36,7 +38,7 @@
     emb, win, wout, gn_sh, inv, hid, act, out, st1, st2, st3, st4, nrm, corr,
     part, far_g, near_gs, near_gr, y_gs, y_gr, gram, go,
     far_s, far_r, near_s, near_r, ys, yr, gact, gh, emb_t,
-    core_s, core_r, own_p, far_is, far_ir, near_is, near_ir, y_is, y_ir, gout,
+    core_r, far_is, far_ir, near_is, near_ir, y_is, y_ir, gout,
     send_sem, recv_sem, local_sem,
 ):
     dp, ft = lax.axis_index("dp"), lax.axis_index("feat")
@@ -61,19 +63,58 @@
     y_next, other = (dp_of(0, 1), ft), (dp_of(0, 0, 1), ft)
     peers = [(lax.rem(dp + k, DP), ft) for k in range(1, DP)]
 
-    started = []
-    counts = [0, 0]
-
-    def send(src, dst, device):
-        i = counts[0]
-        counts[0] += 1
-        copy = pltpu.make_async_remote_copy(
-            src_ref=src, dst_ref=dst, send_sem=send_sem.at[i], recv_sem=recv_sem.at[i],
-            device_id=device, device_id_type=MESH,
-        )
-        copy.start()
-        started.append(copy)
-        return copy
+    waiting = []
+    counts = [0, 0, 0]
+
+    def size(ref):
+        return math.prod(ref.shape) * jnp.dtype(ref.dtype).itemsize
+
+    def all_of(sem, total):
+        count = total // (16 * 2 * WIDE)
+        ref = wout.at[pl.ds(0, 16 * count)]
+        return pltpu.make_async_copy(ref, ref, sem)
+
+    class Sender:
+        def __init__(self):
+            self.sem = send_sem.at[counts[2]]
+            counts[2] += 1
+            self.total = 0
+            senders.append(self)
+
+        def __call__(self, src, dst, device):
+            i = counts[0]
+            counts[0] += 1
+            copy = pltpu.make_async_remote_copy(
+                src_ref=src, dst_ref=dst, send_sem=self.sem, recv_sem=recv_sem.at[i],
+                device_id=device, device_id_type=MESH,
+            )
+            copy.start()
+            self.total += size(src)
+            return copy
+
+        def finish(self):
+            all_of(self.sem, self.total).wait()
+
+    senders = []
+
+    class Share:
+        def __init__(self, table):
+            self.leave, self.land = send_sem.at[counts[2]], recv_sem.at[counts[0]]
+            counts[2] += 1
+            counts[0] += 1
+            for device in peers:
+                pltpu.make_async_remote_copy(
+                    src_ref=table.at[dp], dst_ref=table.at[dp], send_sem=self.leave,
+                    recv_sem=self.land, device_id=device, device_id_type=MESH,
+                ).start()
+            self.others = table.at[pl.ds(0, DP - 1)]
+            senders.append(self)
+
+        def wait_recv(self):
+            pltpu.make_async_copy(self.others, self.others, self.land).wait()
+
+        def finish(self):
+            pltpu.make_async_copy(self.others, self.others, self.leave).wait()
 
     def fetch(src, dst):
         i = counts[1]
@@ -85,7 +126,6 @@
     in_emb = [fetch(emb_a, emb.at[pl.ds(0, ROWS)]), fetch(emb_b, emb.at[pl.ds(ROWS, ROWS)])]
     in_win = fetch(w_in, win)
     in_gs = [fetch(gain, gn_sh.at[pl.ds(0, 1)]), fetch(shift, gn_sh.at[pl.ds(1, 1)])]
-    in_wout = fetch(w_out, wout)
 
     barrier = pltpu.get_barrier_semaphore()
     greeted = peers + [x_right, x_left, y_pair]
@@ -95,19 +135,16 @@
     def rows(v):
         return pl.ds(v * ROWS, ROWS)
 
-    def share(table):
-        return [send(table.at[dp], table.at[dp], device) for device in peers]
-
-    def local_moments(values, table, v, cols):
+    def local_moments(values, table, row, cols):
         center = jnp.sum(values, axis=0, keepdims=True) / ROWS
         spread = jnp.sum((values - center) ** 2, axis=0, keepdims=True)
-        table[dp, 0:1, cols] = center
-        table[dp, 1:2, cols] = spread
-
-    def global_moments(table, cols):
-        centers = table[:, 0, cols]
+        table[dp, row : row + 1, cols] = center
+        table[dp, row + 1 : row + 2, cols] = spread
+
+    def global_moments(table, row, cols):
+        centers = table[:, row, cols]
         center = jnp.sum(centers, axis=0, keepdims=True) / DP
-        spread = jnp.sum(table[:, 1, cols], axis=0, keepdims=True) + ROWS * jnp.sum(
+        spread = jnp.sum(table[:, row + 1, cols], axis=0, keepdims=True) + ROWS * jnp.sum(
             (centers - center) ** 2, axis=0, keepdims=True
         )
         return center, lax.rsqrt(spread / BATCH + epsilon)
@@ -116,28 +153,28 @@
         for copy in in_emb:
             copy.wait()
         in_win.wait()
+        waiting.append(fetch(w_out, wout))
 
         def tile(cols):
             product = jnp.dot(emb[...], win[:, cols], preferred_element_type=f32)
             for v in range(2):
                 piece = product[v * ROWS : (v + 1) * ROWS]
                 hid[v, :, cols] = piece
-                local_moments(piece, st1.at[v], v, cols)
+                local_moments(piece, st1, 2 * v, cols)
 
         column_tiles(tile)
         pl.semaphore_wait(barrier, len(greeted))
 
     def first_norm(v):
-        copies = share(st1.at[v])
-        yield
-        for copy in copies:
-            copy.wait_recv()
         if v == 0:
+            exchange = Share(st1)
+            yield
+            exchange.wait_recv()
             for copy in in_gs:
                 copy.wait()
 
         def tile(cols):
-            center, inverse = global_moments(st1.at[v], cols)
+            center, inverse = global_moments(st1, 2 * v, cols)
             hat = (hid[v, :, cols] - center) * inverse
             hid[v, :, cols] = hat
             inv[v : v + 1, cols] = inverse
@@ -145,6 +182,7 @@
             act[v, ft, :, cols] = jnp.maximum(before, 0.0).astype(bf16)
 
         column_tiles(tile)
+        yield
 
     def project(v, slot, first=False):
         def tile(cols):
@@ -160,6 +198,7 @@
         column_tiles(tile)
 
     def gather_feat(v):
+        send = Sender()
         low, high = pl.ds(0, HALF), pl.ds(HALF, HALF)
         mine, pair = ft, feat_of(0, 1)
 
@@ -171,7 +210,7 @@
         b = go_(mine, x_right)
         c = go_(mine, x_left)
         if v == 0:
-            in_wout.wait()
+            waiting.pop().wait()
         project(v, mine, first=True)
         yield
         a.wait_recv()
@@ -202,14 +241,13 @@
         project(v, feat_of(2, 1))
 
     def second_norm(v):
-        column_tiles(lambda cols: local_moments(out[v, :, cols], st2.at[v], v, cols))
-        copies = share(st2.at[v])
-        yield
-        for copy in copies:
-            copy.wait_recv()
+        column_tiles(lambda cols: local_moments(out[v, :, cols], st2.at[v], 0, cols))
+        exchange = Share(st2.at[v])
+        yield
+        exchange.wait_recv()
 
         def tile(cols):
-            center, inverse = global_moments(st2.at[v], cols)
+            center, inverse = global_moments(st2.at[v], 0, cols)
             hat = (out[v, :, cols] - center) * inverse
             out[v, :, cols] = hat
             inv[2 + v : 3 + v, cols] = inverse
@@ -228,6 +266,7 @@
             )
 
     def gather_dp(v):
+        send = Sender()
         low, high = pl.ds(0, HALF), pl.ds(HALF, HALF)
 
         def go_(slot, device, part_rows=None):
@@ -285,6 +324,7 @@
         from_core(2)
 
     def sum_gram(v):
+        send = Sender()
         low, high = pl.ds(0, BATCH // 2), pl.ds(BATCH // 2, BATCH // 2)
 
         def pair_rows(step):
@@ -385,10 +425,9 @@
             st3[v, dp, 1:2, cols] = jnp.sum(upstream * out[v, :, cols], axis=0, keepdims=True)
 
         column_tiles(tile)
-        copies = share(st3.at[v])
-        yield
-        for copy in copies:
-            copy.wait_recv()
+        exchange = Share(st3.at[v])
+        yield
+        exchange.wait_recv()
 
         def finish(cols):
             up = jnp.sum(st3[v, :, 0, cols], axis=0, keepdims=True) / BATCH
@@ -399,9 +438,18 @@
 
         column_tiles(finish)
 
-    def active_back(v):
+    def keep(ref):
+        def store(cols, value):
+            ref[:, cols] = value.astype(bf16)
+
+        return store
+
+    stores = []
+
+    def active_back(v, h):
+        send = Sender()
         def block(step, flip, store):
-            first = feat_of(step, flip) * WIDE
+            first = feat_of(step, flip) * WIDE + h * PIECE
 
             def tile(cols):
                 store(
@@ -412,38 +460,35 @@
                     ),
                 )
 
-            column_tiles(tile)
+            column_tiles(tile, PIECE)
 
         low, high = pl.ds(0, HALF), pl.ds(HALF, HALF)
 
-        def keep(ref):
-            def store(cols, value):
-                ref[:, cols] = value.astype(bf16)
-
-            return store
-
         def far(flip):
-            block(2, flip, keep(far_s.at[v, flip]))
+            block(2, flip, keep(far_s.at[v, h, flip]))
             return [
-                send(far_s.at[v, flip, low], far_r.at[v, flip, 0], x_right),
-                send(far_s.at[v, flip, high], far_r.at[v, flip, 1], x_left),
+                send(far_s.at[v, h, flip, low], far_r.at[v, h, flip, 0], x_right),
+                send(far_s.at[v, h, flip, high], far_r.at[v, h, flip, 1], x_left),
             ]
 
         def near(flip):
-            block(1, flip, keep(near_s.at[v, flip, 0]))
-            a = send(near_s.at[v, flip, 0, high], near_r.at[v, flip, 0, high], x_right)
-            block(-1, flip, keep(near_s.at[v, flip, 1]))
-            b = send(near_s.at[v, flip, 1, low], near_r.at[v, flip, 1, low], x_left)
+            block(1, flip, keep(near_s.at[v, h, flip, 0]))
+            a = send(near_s.at[v, h, flip, 0, high], near_r.at[v, h, flip, 0, high], x_right)
+            block(-1, flip, keep(near_s.at[v, h, flip, 1]))
+            b = send(near_s.at[v, h, flip, 1, low], near_r.at[v, h, flip, 1, low], x_left)
             return [a, b]
 
         def relay(flip, fars, nears):
             for side, half, device in ((0, low, x_right), (1, high, x_left)):
                 fars[side].wait_recv()
-                near_s[v, flip, side, half] = (
-                    near_s[v, flip, side, half].astype(f32) + far_r[v, flip, side].astype(f32)
+                near_s[v, h, flip, side, half] = (
+                    near_s[v, h, flip, side, half].astype(f32)
+                    + far_r[v, h, flip, side].astype(f32)
                 ).astype(bf16)
                 nears.append(
-                    send(near_s.at[v, flip, side, half], near_r.at[v, flip, side, half], device)
+                    send(
+                        near_s.at[v, h, flip, side, half], near_r.at[v, h, flip, side, half], device
+                    )
                 )
 
         fars1 = far(1)
@@ -453,17 +498,18 @@
         relay(1, fars1, nears1)
         nears0 = near(0)
         yield
+        mine = pl.ds(h * PIECE, PIECE)
 
         def store_own(cols, value):
-            gact[v, :, cols] = value
+            gact[v, :, pl.ds(pl.multiple_of(h * PIECE + cols.start, TILE), TILE)] = value
 
         block(0, 1, store_own)
         for copy in nears1:
             copy.wait_recv()
-        ys[v] = (
-            gact[v] + near_r[v, 1, 0].astype(f32) + near_r[v, 1, 1].astype(f32)
+        ys[v, h] = (
+            gact[v, :, mine] + near_r[v, h, 1, 0].astype(f32) + near_r[v, h, 1, 1].astype(f32)
         ).astype(bf16)
-        last = send(ys.at[v], yr.at[v], y_pair)
+        last = send(ys.at[v, h], yr.at[v, h], y_pair)
         yield
         relay(0, fars0, nears0)
         block(0, 0, store_own)
@@ -471,180 +517,165 @@
         for copy in nears0 + [last]:
             copy.wait_recv()
 
-    def first_back(v):
-        def tile(cols):
-            hat = hid[v, :, cols]
+    def first_back(h):
+        def tile(v, cols):
+            full = pl.ds(pl.multiple_of(h * PIECE + cols.start, TILE), TILE)
+            hat = hid[v, :, full]
             grad = (
-                gact[v, :, cols]
-                + near_r[v, 0, 0, :, cols].astype(f32)
-                + near_r[v, 0, 1, :, cols].astype(f32)
-                + yr[v, :, cols].astype(f32)
+                gact[v, :, full]
+                + near_r[v, h, 0, 0, :, cols].astype(f32)
+                + near_r[v, h, 0, 1, :, cols].astype(f32)
+                + yr[v, h, :, cols].astype(f32)
             )
-            before = gn_sh[0:1, cols] * hat + gn_sh[1:2, cols]
+            before = gn_sh[0:1, full] * hat + gn_sh[1:2, full]
             grad = jnp.where(before > 0, grad, 0.0)
-            gact[v, :, cols] = grad
-            st4[v, dp, 0:1, cols] = jnp.sum(grad, axis=0, keepdims=True)
-            st4[v, dp, 1:2, cols] = jnp.sum(grad * hat, axis=0, keepdims=True)
-
-        column_tiles(tile)
-        copies = share(st4.at[v])
-        yield
-        for copy in copies:
-            copy.wait_recv()
+            gact[v, :, full] = grad
+            st4[h, dp, 2 * v : 2 * v + 1, cols] = jnp.sum(grad, axis=0, keepdims=True)
+            st4[h, dp, 2 * v + 1 : 2 * v + 2, cols] = jnp.sum(grad * hat, axis=0, keepdims=True)
+
+        column_tiles(functools.partial(tile, 1), PIECE)
+        yield
+        column_tiles(functools.partial(tile, 0), PIECE)
+        exchange = Share(st4.at[h])
+        yield
+        exchange.wait_recv()
 
         def finish(cols):
-            up = jnp.sum(st4[v, :, 0, cols], axis=0, keepdims=True)
-            dot = jnp.sum(st4[v, :, 1, cols], axis=0, keepdims=True)
-            gh[rows(v), cols] = (
-                gn_sh[0:1, cols] * inv[v : v + 1, cols]
-                * (gact[v, :, cols] - up / BATCH - hid[v, :, cols] * (dot / BATCH))
-            ).astype(bf16)
-            if v == 0:
-                grad_shift[:, cols] = up
-                grad_gain[:, cols] = dot
-            else:
-                grad_shift[:, cols] += up
-                grad_gain[:, cols] += dot
-
-        column_tiles(finish)
+            full = pl.ds(pl.multiple_of(h * PIECE + cols.start, TILE), TILE)
+            sums = [jnp.sum(st4[h, :, k, cols], axis=0, keepdims=True) for k in range(4)]
+            for v in range(2):
+                up, dot = sums[2 * v], sums[2 * v + 1]
+                gh[rows(v), full] = (
+                    gn_sh[0:1, full] * inv[v : v + 1, full]
+                    * (gact[v, :, full] - up / BATCH - hid[v, :, full] * (dot / BATCH))
+                ).astype(bf16)
+            grad_shift[:, full] = sums[0] + sums[2]
+            grad_gain[:, full] = sums[1] + sums[3]
+
+        column_tiles(finish, PIECE)
 
     def transpose_emb():
         for k in range(EMB // ROWS):
             cols = slice(k * ROWS, (k + 1) * ROWS)
             emb_t[cols, :] = emb[:, cols].T
 
-    def last_layer():
+    def last_layer(h):
+        send = Sender()
         low, high = pl.ds(0, OUT // 2), pl.ds(OUT // 2, OUT // 2)
-
-        def partial(step, flip_y, flip_core, store):
+        mine = pl.ds(h * PIECE, PIECE)
+
+        def product(cols):
+            full = pl.ds(pl.multiple_of(h * PIECE + cols.start, TILE), TILE)
+            win[:, full] = jnp.dot(
+                emb_t[...], gh[:, full], preferred_element_type=f32
+            ).astype(bf16)
+
+        def block(step, flip_y, flip_core):
             target = dp_of(step, flip_y, flip_core)
-            left = emb_t[pl.ds(pl.multiple_of(target * OUT, OUT), OUT), :]
-            column_tiles(
-                lambda cols: store(
-                    cols, jnp.dot(left, gh[:, cols], preferred_element_type=f32)
-                )
-            )
-
+            return win.at[pl.ds(pl.multiple_of(target * OUT, OUT), OUT), mine]
+
+        column_tiles(product, PIECE)
         order = [(2, 1), (1, 1), (-1, 1), (2, 0), (1, 0), (-1, 0), (0, 1), (0, 0)]
         crossing = {}
         for n, (step, flip) in enumerate(order):
-            def store(cols, value, n=n):
-                core_s[n, :, cols] = value.astype(bf16)
-
-            partial(step, flip, 1, store)
-            crossing[step, flip] = send(core_s.at[n], core_r.at[n], other)
-
-        def chip_sum(step, flip, keep):
+            crossing[step, flip] = send(block(step, flip, 1), core_r.at[h, n], other)
+        yield
+
+        def chip_sum(step, flip):
             n = order.index((step, flip))
-
-            def store(cols, value):
-                own_p[n, :, cols] = value
-
-            partial(step, flip, 0, store)
             crossing[step, flip].wait_recv()
-
-            def tile(cols):
-                keep(cols, own_p[n, :, cols] + core_r[n, :, cols].astype(f32))
-
-            column_tiles(tile)
-
-        def keep(ref):
-            def store(cols, value):
-                ref[:, cols] = value.astype(bf16)
-
-            return store
+            return block(step, flip, 0)[...].astype(f32) + core_r[h, n].astype(f32)
 
         def far(flip):
-            chip_sum(2, flip, keep(far_is.at[flip]))
+            far_is[h, flip] = chip_sum(2, flip).astype(bf16)
             return [
-                send(far_is.at[flip, low], far_ir.at[flip, 0], z_right),
-                send(far_is.at[flip, high], far_ir.at[flip, 1], z_left),
+                send(far_is.at[h, flip, low], far_ir.at[h, flip, 0], z_right),
+                send(far_is.at[h, flip, high], far_ir.at[h, flip, 1], z_left),
             ]
 
         def near(flip):
-            chip_sum(1, flip, keep(near_is.at[flip, 0]))
-            a = send(near_is.at[flip, 0, high], near_ir.at[flip, 0, high], z_right)
-            chip_sum(-1, flip, keep(near_is.at[flip, 1]))
-            b = send(near_is.at[flip, 1, low], near_ir.at[flip, 1, low], z_left)
+            near_is[h, flip, 0] = chip_sum(1, flip).astype(bf16)
+            a = send(near_is.at[h, flip, 0, high], near_ir.at[h, flip, 0, high], z_right)
+            near_is[h, flip, 1] = chip_sum(-1, flip).astype(bf16)
+            b = send(near_is.at[h, flip, 1, low], near_ir.at[h, flip, 1, low], z_left)
             return [a, b]
 
         def relay(flip, fars, nears):
             for side, half, device in ((0, low, z_right), (1, high, z_left)):
                 fars[side].wait_recv()
-                near_is[flip, side, half] = (
-                    near_is[flip, side, half].astype(f32) + far_ir[flip, side].astype(f32)
+                near_is[h, flip, side, half] = (
+                    near_is[h, flip, side, half].astype(f32) + far_ir[h, flip, side].astype(f32)
                 ).astype(bf16)
                 nears.append(
-                    send(near_is.at[flip, side, half], near_ir.at[flip, side, half], device)
+                    send(near_is.at[h, flip, side, half], near_ir.at[h, flip, side, half], device)
                 )
 
-        def line_sum(flip, store):
-            n = order.index((0, flip))
-
-            def tile(cols):
-                store(
-                    cols,
-                    own_p[n, :, cols]
-                    + near_ir[flip, 0, :, cols].astype(f32)
-                    + near_ir[flip, 1, :, cols].astype(f32),
-                )
-
-            column_tiles(tile)
+        def line_sum(flip):
+            return (
+                chip_sum(0, flip)
+                + near_ir[h, flip, 0].astype(f32)
+                + near_ir[h, flip, 1].astype(f32)
+            )
 
         fars1 = far(1)
         nears1 = near(1)
+        yield
         fars0 = far(0)
         relay(1, fars1, nears1)
         nears0 = near(0)
-
-        def own(flip):
-            n = order.index((0, flip))
-
-            def store(cols, value):
-                own_p[n, :, cols] = value
-
-            chip_sum(0, flip, store)
-
-        own(1)
+        yield
         for copy in nears1:
             copy.wait_recv()
-        line_sum(1, keep(y_is))
-        last = send(y_is, y_ir, y_next)
+        y_is[h] = line_sum(1).astype(bf16)
+        last = send(y_is.at[h], y_ir.at[h], y_next)
         relay(0, fars0, nears0)
-        own(0)
+        yield
         for copy in nears0 + [last]:
             copy.wait_recv()
-
-        def finish(cols, value):
-            gout[:, cols] = value + y_ir[:, cols].astype(f32)
-
-        line_sum(0, finish)
-        store_out = fetch(gout, grad_in)
-        store_out.wait()
-
-    def together(*stages):
-        stages = list(stages)
-        while stages:
-            for stage in list(stages):
-                if next(stage, True):
-                    stages.remove(stage)
-
-    both = lambda stage: together(stage(0), stage(1))
+        gout[:, mine] = line_sum(0) + y_ir[h].astype(f32)
+        stores.append(fetch(gout.at[:, mine], grad_in.at[:, mine]))
+
+    def once(stage, *args):
+        stage(*args)
+        yield
+
+    first_a, first_b = first_norm(0), first_norm(1)
+    feat_a, feat_b = gather_feat(0), gather_feat(1)
+    norm_a, norm_b = second_norm(0), second_norm(1)
+    dp_a, dp_b = gather_dp(0), gather_dp(1)
+    gram_a, gram_b = sum_gram(0), sum_gram(1)
+    back_a, back_b = output_back(0), output_back(1)
+    act_a0, act_a1, act_b0, act_b1 = (active_back(v, h) for v in range(2) for h in range(2))
+    pre_0, pre_1 = first_back(0), first_back(1)
+    last_0, last_1 = last_layer(0), last_layer(1)
+    loss, row = once(losses), once(row_losses)
+    turn = once(transpose_emb)
+    order = (
+        first_a, first_a, feat_a, first_b, turn, feat_a, feat_a, feat_a, feat_b,
+        feat_a, feat_a, norm_a, feat_b, norm_a, dp_a, feat_b, dp_a, feat_b, dp_a, feat_b, feat_b,
+        norm_b, dp_a, norm_b, dp_a, dp_b, dp_a, gram_a, dp_b, gram_a, dp_b, gram_a, dp_b,
+        gram_a, gram_a, dp_b, gram_a, gram_a, dp_b, loss,
+        gram_b, back_b, gram_b, back_b, act_b0, gram_b, gram_b, gram_b, act_b0, gram_b, gram_b,
+        back_a, act_b0, act_b1, back_a, act_b0, act_a0, act_b1, act_b0, act_b1, pre_0, act_a0,
+        act_b1, act_a0, act_a1, act_b1, act_a0, act_a1, act_a0, pre_0, pre_1, act_a1, pre_0,
+        last_0, act_a1, last_0, row, act_a1, pre_1, last_0, last_0, pre_1, last_1, last_0,
+        last_1, last_1, last_1, last_1,
+    )
     first_layer()
-    both(first_norm)
-    transpose_emb()
-    both(gather_feat)
-    both(second_norm)
-    both(gather_dp)
-    losses()
-    both(sum_gram)
-    both(output_back)
-    row_losses()
-    both(active_back)
-    both(first_back)
-    last_layer()
-    for copy in started:
-        copy.wait_send()
+    for stage in order:
+        next(stage, None)
+    for stage in order:
+        for _ in stage:
+            raise ValueError()
+    for copy in stores:
+        copy.wait()
+    for sender in senders:
+        sender.finish()
+
+
+def copies(*refs):
+    for i in range(5):
+        refs[5 + i][...] = refs[i][...]
 
 
 def scratch():
@@ -653,22 +684,22 @@
         v((2 * ROWS, EMB), bf16), v((EMB, WIDE), bf16), v((FEAT * WIDE, WIDE), bf16),
         v((2, WIDE), f32), v((4, WIDE), f32), v((2, ROWS, WIDE), f32), v((2, FEAT, ROWS, WIDE), bf16),
         v((2, ROWS, WIDE), f32),
-        v((2, DP, 2, WIDE), f32), v((2, DP, 2, WIDE), f32),
-        v((2, DP, 2, WIDE), f32), v((2, DP, 2, WIDE), f32),
+        v((DP, 4, WIDE), f32), v((2, DP, 2, WIDE), f32),
+        v((2, DP, 2, WIDE), f32), v((2, DP, 4, PIECE), f32),
         v((2, DP, ROWS, WIDE), bf16), v((DP, WIDE), f32),
         v((2, ROWS, BATCH), bf16), v((2, 2, 32, BATCH // 2), bf16),
         v((2, 2, 32, BATCH), bf16), v((2, 2, 32, BATCH), bf16),
         v((2, 16, BATCH), bf16), v((2, 16, BATCH), bf16), v((2, ROWS, BATCH), bf16),
         v((2, ROWS, WIDE), bf16),
-        v((2, 2, ROWS, WIDE), bf16), v((2, 2, 2, HALF, WIDE), bf16),
-        v((2, 2, 2, ROWS, WIDE), bf16), v((2, 2, 2, ROWS, WIDE), bf16),
-        v((2, ROWS, WIDE), bf16), v((2, ROWS, WIDE), bf16), v((2, ROWS, WIDE), f32),
+        v((2, 2, 2, ROWS, PIECE), bf16), v((2, 2, 2, 2, HALF, PIECE), bf16),
+        v((2, 2, 2, 2, ROWS, PIECE), bf16), v((2, 2, 2, 2, ROWS, PIECE), bf16),
+        v((2, 2, ROWS, PIECE), bf16), v((2, 2, ROWS, PIECE), bf16), v((2, ROWS, WIDE), f32),
         v((2 * ROWS, WIDE), bf16), v((EMB, 2 * ROWS), bf16),
-        v((8, OUT, WIDE), bf16), v((8, OUT, WIDE), bf16), v((8, OUT, WIDE), f32),
-        v((2, OUT, WIDE), bf16), v((2, 2, OUT // 2, WIDE), bf16),
-        v((2, 2, OUT, WIDE), bf16), v((2, 2, OUT, WIDE), bf16),
-        v((OUT, WIDE), bf16), v((OUT, WIDE), bf16), v((OUT, WIDE), f32),
-        pltpu.SemaphoreType.DMA((260,)), pltpu.SemaphoreType.DMA((260,)),
+        v((2, 8, OUT, PIECE), bf16),
+        v((2, 2, OUT, PIECE), bf16), v((2, 2, 2, OUT // 2, PIECE), bf16),
+        v((2, 2, 2, OUT, PIECE), bf16), v((2, 2, 2, OUT, PIECE), bf16),
+        v((2, OUT, PIECE), bf16), v((2, OUT, PIECE), bf16), v((OUT, WIDE), f32),
+        pltpu.SemaphoreType.DMA((20,)), pltpu.SemaphoreType.DMA((186,)),
         pltpu.SemaphoreType.DMA((8,)),
     ]
 
@@ -693,6 +724,12 @@
         ),
         cost_estimate=pl.CostEstimate(flops=14 * 10**9, bytes_accessed=24 * 2**20, transcendentals=0),
     )(emb_a, emb_b, w_in, w_out, gain.reshape(1, WIDE), shift.reshape(1, WIDE))
+    results = pl.pallas_call(
+        copies,
+        out_shape=tuple(jax.ShapeDtypeStruct(r.shape, r.dtype) for r in results),
+        in_specs=[near] * 5,
+        out_specs=(near,) * 5,
+    )(*results)
     return (results[0],) + tuple(r.reshape(-1) for r in results[1:])
 
 

time: 211 us -> 186 us (0.88)
  Pallas kernels: 203 us -> 185 us
  local copies, waits for them, and re-layouts: 6.75 us -> 0 us
    pallas_call x1, Pallas kernels: 203 us -> 184 us  [shards(): pl.pallas_call(kernel, out_shape=(jax.ShapeDtypeStruct((OUT, WIDE), f32),...]
    unnamed x5 -> x0, local copies, waits for them, and re-layouts: 6.75 us -> none
where the time goes in v2:
time: 186 us
  Pallas kernels  185 us (99%)
    pallas_call x1, Pallas kernels, shards(): pl.pallas_call(kernel, out_shape=(jax.ShapeDtypeStruct((OUT, WIDE), f32),...  184 us

profile of v2, /device:TPU:0, one launch (start us, length us, event | category | flops | bytes accessed | tf_op | source)
XLA Modules:
  0.0 186.0 jit_solution(8982726643347751579)
XLA Ops:
  0.6 183.5 %shard_map.101 = (f32[96,1024]{1,0:T(8,128)}, f32[1,1024]{1,0:T(1,128)}, f32[1,1024]{1,0:T(1,128)}, f32[1,1024]{1,0:T(1,128)}, f32[1,128]{1,0:T(1,128)}) custom-call(bf16[128,1536]{1,0:T(8,128)(2,1)} %emb_a.1, bf16[128,1536]{1,0:T(8,128)(2,1)} %emb_b.1, bf16[1536,1024]{1,0:T(8,128)(2,1)} %w_in.1, bf16[8192,1024]{1,0:T(8,128)(2,1)} %w_out.1, ...), custom_call_target="tpu_custom_call" | custom-call | flops 14000000000 | bytes 25165824 | tf_op jit(solution)/shard_map/pallas_call | solution.py:710
  184.2 1.8 shard_map.102

commit v3 on v2

--- a/solution.py
+++ b/solution.py
@@ -21,6 +21,9 @@
 TILE = 256
 PIECE = WIDE // 2
 HALF = ROWS // 2
+FEAT_EDGE = (HALF, HALF)
+DP_EDGE = (HALF, HALF)
+BACK_EDGE = ((48, 48), (48, 48))
 f32 = jnp.float32
 bf16 = jnp.bfloat16
 NT = (((1,), (1,)), ((), ()))
@@ -37,7 +40,7 @@
     grad_in, grad_gain, grad_shift, diag_loss, row_loss,
     emb, win, wout, gn_sh, inv, hid, act, out, st1, st2, st3, st4, nrm, corr,
     part, far_g, near_gs, near_gr, y_gs, y_gr, gram, go,
-    far_s, far_r, near_s, near_r, ys, yr, gact, gh, emb_t,
+    far_s, far_r, near_s, near_r, ys, yr, cross_s, cross_r, gact, gh, emb_t,
     core_r, far_is, far_ir, near_is, near_ir, y_is, y_ir, gout,
     send_sem, recv_sem, local_sem,
 ):
@@ -197,48 +200,66 @@
 
         column_tiles(tile)
 
-    def gather_feat(v):
+    def gather(buffer, slot, right, left, pair, edge, have):
         send = Sender()
         low, high = pl.ds(0, HALF), pl.ds(HALF, HALF)
-        mine, pair = ft, feat_of(0, 1)
-
-        def go_(slot, device, part_rows=None):
-            ref = act.at[v, slot] if part_rows is None else act.at[v, slot, part_rows]
+        top, bottom = pl.ds(0, edge), pl.ds(ROWS - edge, edge)
+        middle = pl.ds(edge, ROWS - 2 * edge)
+        split = edge < HALF
+
+        def go_(block, device, part_rows=None):
+            ref = buffer.at[block] if part_rows is None else buffer.at[block, part_rows]
             return send(ref, ref, device)
 
-        a = go_(mine, y_pair)
-        b = go_(mine, x_right)
-        c = go_(mine, x_left)
-        if v == 0:
-            waiting.pop().wait()
-        project(v, mine, first=True)
-        yield
-        a.wait_recv()
-        d = go_(pair, x_right)
-        e = go_(pair, x_left)
-        project(v, pair)
-        yield
-        b.wait_recv()
-        f = go_(feat_of(-1), x_right, low)
-        c.wait_recv()
-        g = go_(feat_of(1), x_left, high)
-        project(v, feat_of(-1))
-        project(v, feat_of(1))
-        yield
-        d.wait_recv()
-        h = go_(feat_of(-1, 1), x_right, low)
-        e.wait_recv()
-        i = go_(feat_of(1, 1), x_left, high)
-        project(v, feat_of(-1, 1))
-        project(v, feat_of(1, 1))
-        yield
-        f.wait_recv()
-        g.wait_recv()
-        project(v, feat_of(2))
-        yield
-        h.wait_recv()
-        i.wait_recv()
-        project(v, feat_of(2, 1))
+        def arrive(*copies):
+            for copy in copies:
+                copy.wait_recv()
+
+        a = go_(slot(0, 0), pair)
+        b = go_(slot(0, 0), right)
+        c = go_(slot(0, 0), left)
+        have(0, 0)
+        yield
+        arrive(a)
+        parts = (top, bottom) if split else (None,)
+        d = [go_(slot(0, 1), right, part_rows) for part_rows in parts]
+        e = [go_(slot(0, 1), left, part_rows) for part_rows in parts[::-1]]
+        have(0, 1)
+        yield
+        late = []
+        arrive(b)
+        f = go_(slot(-1, 0), right, low)
+        if split:
+            late.append(go_(slot(-1, 0), pair, middle))
+        arrive(c)
+        g = go_(slot(1, 0), left, high)
+        if split:
+            late.append(go_(slot(1, 0), pair, middle))
+        have(-1, 0)
+        have(1, 0)
+        yield
+        arrive(d[0])
+        h = go_(slot(-1, 1), right, top)
+        arrive(e[0])
+        i = go_(slot(1, 1), left, bottom)
+        arrive(*d[1:], *e[1:], *late)
+        have(-1, 1)
+        have(1, 1)
+        yield
+        arrive(f, g)
+        late = [go_(slot(2, 0), pair, middle)] if split else []
+        have(2, 0)
+        yield
+        arrive(h, i, *late)
+        have(2, 1)
+
+    def gather_feat(v):
+        def have(step, flip):
+            if v == 0 and waiting:
+                waiting.pop().wait()
+            project(v, feat_of(step, flip), first=step == 0 and flip == 0)
+
+        return gather(act.at[v], feat_of, x_right, x_left, y_pair, FEAT_EDGE[v], have)
 
     def second_norm(v):
         column_tiles(lambda cols: local_moments(out[v, :, cols], st2.at[v], 0, cols))
@@ -267,18 +288,7 @@
 
     def gather_dp(v):
         send = Sender()
-        low, high = pl.ds(0, HALF), pl.ds(HALF, HALF)
-
-        def go_(slot, device, part_rows=None):
-            ref = nrm.at[v, slot] if part_rows is None else nrm.at[v, slot, part_rows]
-            return send(ref, ref, device)
-
         cores = []
-
-        def have(step, flip):
-            slot = dp_of(step, flip)
-            cores.append((go_(slot, other), step, flip))
-            inner(v, slot)
 
         def from_core(count):
             for _ in range(count):
@@ -286,42 +296,14 @@
                 copy.wait_recv()
                 inner(v, dp_of(step, flip, 1))
 
-        a = go_(dp, y_next)
-        b = go_(dp, z_right)
-        c = go_(dp, z_left)
-        have(0, 0)
-        yield
-        a.wait_recv()
-        d = go_(dp_of(0, 1), z_right)
-        e = go_(dp_of(0, 1), z_left)
-        have(0, 1)
-        from_core(1)
-        yield
-        b.wait_recv()
-        f = go_(dp_of(-1), z_right, low)
-        c.wait_recv()
-        g = go_(dp_of(1), z_left, high)
-        have(-1, 0)
-        have(1, 0)
-        from_core(1)
-        yield
-        d.wait_recv()
-        h = go_(dp_of(-1, 1), z_right, low)
-        e.wait_recv()
-        i = go_(dp_of(1, 1), z_left, high)
-        have(-1, 1)
-        have(1, 1)
-        from_core(2)
-        yield
-        f.wait_recv()
-        g.wait_recv()
-        have(2, 0)
-        from_core(2)
-        yield
-        h.wait_recv()
-        i.wait_recv()
-        have(2, 1)
-        from_core(2)
+        def have(step, flip):
+            slot = dp_of(step, flip)
+            cores.append((send(nrm.at[v, slot], nrm.at[v, slot], other), step, flip))
+            inner(v, slot)
+            if (step, flip) not in ((0, 0), (-1, 0), (-1, 1)):
+                from_core(len(cores) if (step, flip) == (2, 1) else len(cores) - 1)
+
+        return gather(nrm.at[v], dp_of, z_right, z_left, y_next, DP_EDGE[v], have)
 
     def sum_gram(v):
         send = Sender()
@@ -383,6 +365,7 @@
         a.wait_recv()
         d = go_(slot(0, 1), x_right)
         e = go_(slot(0, 1), x_left)
+        yield
         b.wait_recv()
         f = go_(slot(-1), x_right, low)
         c.wait_recv()
@@ -462,70 +445,126 @@
 
             column_tiles(tile, PIECE)
 
+        edge = BACK_EDGE[v][h]
+        top, bottom = pl.ds(0, edge), pl.ds(ROWS - edge, edge)
+        middle, between = pl.ds(edge, ROWS - 2 * edge), pl.ds(0, ROWS - 2 * edge)
+        mine = pl.ds(h * PIECE, PIECE)
+        crossed = {}
+
+        def cross(step, ref):
+            slot = (2, 1, -1, 0).index(step)
+            crossed[step] = send(ref, cross_r.at[v, h, slot, between], y_pair)
+
+        def added(step, ref):
+            slot = (2, 1, -1, 0).index(step)
+            crossed[step].wait_recv()
+
+            def store(cols, value):
+                ref[:, cols] = value.astype(bf16)
+                ref[middle, cols] = (
+                    value[edge : ROWS - edge] + cross_r[v, h, slot, between, cols].astype(f32)
+                ).astype(bf16)
+
+            return store
+
+        def far(flip):
+            ref = far_s.at[v, h, flip]
+            block(2, flip, keep(ref) if flip else added(2, ref))
+            if flip:
+                cross(2, ref.at[middle])
+            first, second = (top, bottom) if flip else (low, high)
+            into = between_half if not flip else pl.ds(0, edge)
+            return [
+                send(ref.at[first], far_r.at[v, h, flip, 0, into], x_right),
+                send(ref.at[second], far_r.at[v, h, flip, 1, into], x_left),
+            ]
+
         low, high = pl.ds(0, HALF), pl.ds(HALF, HALF)
-
-        def far(flip):
-            block(2, flip, keep(far_s.at[v, h, flip]))
-            return [
-                send(far_s.at[v, h, flip, low], far_r.at[v, h, flip, 0], x_right),
-                send(far_s.at[v, h, flip, high], far_r.at[v, h, flip, 1], x_left),
-            ]
+        between_half = pl.ds(0, HALF)
 
         def near(flip):
-            block(1, flip, keep(near_s.at[v, h, flip, 0]))
-            a = send(near_s.at[v, h, flip, 0, high], near_r.at[v, h, flip, 0, high], x_right)
-            block(-1, flip, keep(near_s.at[v, h, flip, 1]))
-            b = send(near_s.at[v, h, flip, 1, low], near_r.at[v, h, flip, 1, low], x_left)
-            return [a, b]
+            first, second = (top, bottom) if flip else (low, high)
+            copies = []
+            for side, step, part_rows, device in ((0, 1, second, x_right), (1, -1, first, x_left)):
+                ref = near_s.at[v, h, flip, side]
+                block(step, flip, keep(ref) if flip else added(step, ref))
+                copies.append(
+                    send(ref.at[part_rows], near_r.at[v, h, flip, side, part_rows], device)
+                )
+                if flip:
+                    cross(step, ref.at[middle])
+            return copies
 
         def relay(flip, fars, nears):
-            for side, half, device in ((0, low, x_right), (1, high, x_left)):
+            first, second = (top, bottom) if flip else (low, high)
+            into = between_half if not flip else pl.ds(0, edge)
+            for side, part_rows, device in ((0, first, x_right), (1, second, x_left)):
                 fars[side].wait_recv()
-                near_s[v, h, flip, side, half] = (
-                    near_s[v, h, flip, side, half].astype(f32)
-                    + far_r[v, h, flip, side].astype(f32)
+                near_s[v, h, flip, side, part_rows] = (
+                    near_s[v, h, flip, side, part_rows].astype(f32)
+                    + far_r[v, h, flip, side, into].astype(f32)
                 ).astype(bf16)
                 nears.append(
                     send(
-                        near_s.at[v, h, flip, side, half], near_r.at[v, h, flip, side, half], device
+                        near_s.at[v, h, flip, side, part_rows],
+                        near_r.at[v, h, flip, side, part_rows], device,
                     )
                 )
 
-        fars1 = far(1)
-        nears1 = near(1)
-        yield
-        fars0 = far(0)
-        relay(1, fars1, nears1)
-        nears0 = near(0)
-        yield
-        mine = pl.ds(h * PIECE, PIECE)
-
         def store_own(cols, value):
             gact[v, :, pl.ds(pl.multiple_of(h * PIECE + cols.start, TILE), TILE)] = value
 
-        block(0, 1, store_own)
+        def store_pair(cols, value):
+            store_own(cols, value)
+            cross_s[v, h, between, cols] = value[edge : ROWS - edge].astype(bf16)
+
+        fars1 = far(1)
+        yield
+        nears1 = near(1)
+        yield
+        block(0, 1, store_pair)
+        cross(0, cross_s.at[v, h, between])
+        yield
+        fars0 = far(0)
+        yield
+        relay(1, fars1, nears1)
+        yield
+        nears0 = near(0)
+        yield
         for copy in nears1:
             copy.wait_recv()
-        ys[v, h] = (
-            gact[v, :, mine] + near_r[v, h, 1, 0].astype(f32) + near_r[v, h, 1, 1].astype(f32)
-        ).astype(bf16)
-        last = send(ys.at[v, h], yr.at[v, h], y_pair)
+        for place, part_rows in ((pl.ds(0, edge), top), (pl.ds(edge, edge), bottom)):
+            ys[v, h, place] = (
+                gact[v, part_rows, mine]
+                + near_r[v, h, 1, 0, part_rows].astype(f32)
+                + near_r[v, h, 1, 1, part_rows].astype(f32)
+            ).astype(bf16)
+        edges = pl.ds(0, 2 * edge)
+        last = send(ys.at[v, h, edges], yr.at[v, h, edges], y_pair)
+        yield
+        block(0, 0, store_own)
         yield
         relay(0, fars0, nears0)
-        block(0, 0, store_own)
-        yield
-        for copy in nears0 + [last]:
+        yield
+        for copy in nears0 + [last, crossed[0]]:
             copy.wait_recv()
 
     def first_back(h):
         def tile(v, cols):
+            edge = BACK_EDGE[v][h]
             full = pl.ds(pl.multiple_of(h * PIECE + cols.start, TILE), TILE)
             hat = hid[v, :, full]
             grad = (
                 gact[v, :, full]
                 + near_r[v, h, 0, 0, :, cols].astype(f32)
                 + near_r[v, h, 0, 1, :, cols].astype(f32)
-                + yr[v, h, :, cols].astype(f32)
+                + jnp.concatenate(
+                    [
+                        yr[v, h, 0:edge, cols],
+                        cross_r[v, h, 3, 0 : ROWS - 2 * edge, cols],
+                        yr[v, h, edge : 2 * edge, cols],
+                    ]
+                ).astype(f32)
             )
             before = gn_sh[0:1, full] * hat + gn_sh[1:2, full]
             grad = jnp.where(before > 0, grad, 0.0)
@@ -621,13 +660,16 @@
         nears1 = near(1)
         yield
         fars0 = far(0)
+        yield
         relay(1, fars1, nears1)
+        yield
         nears0 = near(0)
         yield
         for copy in nears1:
             copy.wait_recv()
         y_is[h] = line_sum(1).astype(bf16)
         last = send(y_is.at[h], y_ir.at[h], y_next)
+        yield
         relay(0, fars0, nears0)
         yield
         for copy in nears0 + [last]:
@@ -651,15 +693,16 @@
     loss, row = once(losses), once(row_losses)
     turn = once(transpose_emb)
     order = (
-        first_a, first_a, feat_a, first_b, turn, feat_a, feat_a, feat_a, feat_b,
-        feat_a, feat_a, norm_a, feat_b, norm_a, dp_a, feat_b, dp_a, feat_b, dp_a, feat_b, feat_b,
-        norm_b, dp_a, norm_b, dp_a, dp_b, dp_a, gram_a, dp_b, gram_a, dp_b, gram_a, dp_b,
-        gram_a, gram_a, dp_b, gram_a, gram_a, dp_b, loss,
-        gram_b, back_b, gram_b, back_b, act_b0, gram_b, gram_b, gram_b, act_b0, gram_b, gram_b,
-        back_a, act_b0, act_b1, back_a, act_b0, act_a0, act_b1, act_b0, act_b1, pre_0, act_a0,
-        act_b1, act_a0, act_a1, act_b1, act_a0, act_a1, act_a0, pre_0, pre_1, act_a1, pre_0,
-        last_0, act_a1, last_0, row, act_a1, pre_1, last_0, last_0, pre_1, last_1, last_0,
-        last_1, last_1, last_1, last_1,
+        first_a, first_a, feat_a, feat_a, first_b, feat_a, feat_a, feat_b, feat_a, turn, feat_a,
+        norm_a, feat_b, norm_a, dp_a, feat_b, feat_b, dp_a, dp_a, feat_b, feat_b, norm_b, dp_a,
+        dp_a, norm_b, dp_b, dp_a, gram_a, gram_a, dp_b, gram_a, dp_b, gram_a, dp_b, gram_a, dp_b,
+        dp_b, gram_b, gram_a, gram_b, loss, gram_a, gram_b, gram_a, back_b, gram_b, back_b, act_b1,
+        gram_b, act_b0, act_b0, act_b1, gram_b, act_b0, act_b1, gram_b, act_b1, act_b1, act_b0,
+        act_b0, act_b0, act_b1, gram_b, back_a, act_b1, act_b1, act_b1, act_b0, act_b0, act_b0,
+        back_a, act_a1, act_a0, act_a1, act_a0, act_b1, act_a0, act_a1, act_a1, act_a1, act_a0,
+        act_a0, act_b0, row, act_a1, pre_1, act_a1, act_a1, act_a1, act_a0, act_a0, act_a0, act_a0,
+        act_a1, pre_1, pre_0, act_a0, pre_0, pre_1, last_1, pre_0, last_1, last_0, last_1, last_0,
+        last_1, last_0, last_0, last_1, last_0, last_1, last_1, last_0, last_0, last_1, last_0,
     )
     first_layer()
     for stage in order:
@@ -693,13 +736,14 @@
         v((2, ROWS, WIDE), bf16),
         v((2, 2, 2, ROWS, PIECE), bf16), v((2, 2, 2, 2, HALF, PIECE), bf16),
         v((2, 2, 2, 2, ROWS, PIECE), bf16), v((2, 2, 2, 2, ROWS, PIECE), bf16),
-        v((2, 2, ROWS, PIECE), bf16), v((2, 2, ROWS, PIECE), bf16), v((2, ROWS, WIDE), f32),
+        v((2, 2, ROWS, PIECE), bf16), v((2, 2, ROWS, PIECE), bf16),
+        v((2, 2, HALF, PIECE), bf16), v((2, 2, 4, HALF, PIECE), bf16), v((2, ROWS, WIDE), f32),
         v((2 * ROWS, WIDE), bf16), v((EMB, 2 * ROWS), bf16),
         v((2, 8, OUT, PIECE), bf16),
         v((2, 2, OUT, PIECE), bf16), v((2, 2, 2, OUT // 2, PIECE), bf16),
         v((2, 2, 2, OUT, PIECE), bf16), v((2, 2, 2, OUT, PIECE), bf16),
         v((2, OUT, PIECE), bf16), v((2, OUT, PIECE), bf16), v((OUT, WIDE), f32),
-        pltpu.SemaphoreType.DMA((20,)), pltpu.SemaphoreType.DMA((186,)),
+        pltpu.SemaphoreType.DMA((21,)), pltpu.SemaphoreType.DMA((216,)),
         pltpu.SemaphoreType.DMA((8,)),
     ]
 

time: 186 us -> 163 us (0.88)
  Pallas kernels: 185 us -> 162 us
    pallas_call x1, Pallas kernels: 184 us -> 160 us  [shards(): pl.pallas_call(kernel, out_shape=(jax.ShapeDtypeStruct((OUT, WIDE), f32),...]
where the time goes in v3:
time: 163 us
  Pallas kernels  162 us (99%)
    pallas_call x1, Pallas kernels, shards(): pl.pallas_call(kernel, out_shape=(jax.ShapeDtypeStruct((OUT, WIDE), f32),...  160 us

profile of v3, /device:TPU:0, one launch (start us, length us, event | category | flops | bytes accessed | tf_op | source)
XLA Modules:
  0.0 162.6 jit_solution(17030046252372719062)
XLA Ops:
  0.6 160.1 %shard_map.101 = (f32[96,1024]{1,0:T(8,128)}, f32[1,1024]{1,0:T(1,128)}, f32[1,1024]{1,0:T(1,128)}, f32[1,1024]{1,0:T(1,128)}, f32[1,128]{1,0:T(1,128)}) custom-call(bf16[128,1536]{1,0:T(8,128)(2,1)} %emb_a.1, bf16[128,1536]{1,0:T(8,128)(2,1)} %emb_b.1, bf16[1536,1024]{1,0:T(8,128)(2,1)} %w_in.1, bf16[8192,1024]{1,0:T(8,128)(2,1)} %w_out.1, ...), custom_call_target="tpu_custom_call" | custom-call | flops 14000000000 | bytes 25165824 | tf_op jit(solution)/shard_map/pallas_call | solution.py:754
  160.8 1.8 %shard_map.102 = (f32[96,1024]{1,0:T(8,128)}, f32[1,1024]{1,0:T(1,128)}, f32[1,1024]{1,0:T(1,128)}, f32[1,1024]{1,0:T(1,128)}, f32[1,128]{1,0:T(1,128)}) custom-call(f32[96,1024]{1,0:T(8,128)} %get-tuple-element.15.refs_0_, f32[1,1024]{1,0:T(1,128)} %get-tuple-element.16.refs_1_, f32[1,1024]{1,0:T(1,128)} %get-tuple-element.17.refs_2_, ...), custom_call_target="tpu_custom_call" | custom-call | tf_op jit(solution)/shard_map/pallas_call | solution.py:771

commit v4 on v3

--- a/solution.py
+++ b/solution.py
@@ -19,7 +19,9 @@
 FEAT = 8
 OUT = EMB // DP
 TILE = 256
-PIECE = WIDE // 2
+PIECES = (512, 512)
+STARTS = (0, 512)
+PIECE = max(PIECES)
 HALF = ROWS // 2
 FEAT_EDGE = (HALF, HALF)
 DP_EDGE = (HALF, HALF)
@@ -39,7 +41,7 @@
     emb_a, emb_b, w_in, w_out, gain, shift,
     grad_in, grad_gain, grad_shift, diag_loss, row_loss,
     emb, win, wout, gn_sh, inv, hid, act, out, st1, st2, st3, st4, nrm, corr,
-    part, far_g, near_gs, near_gr, y_gs, y_gr, gram, go,
+    part, sum_r, gram, go,
     far_s, far_r, near_s, near_r, ys, yr, cross_s, cross_r, gact, gh, emb_t,
     core_r, far_is, far_ir, near_is, near_ir, y_is, y_ir, gout,
     send_sem, recv_sem, local_sem,
@@ -65,6 +67,8 @@
     z_right, z_left = (dp_of(1), ft), (dp_of(-1), ft)
     y_next, other = (dp_of(0, 1), ft), (dp_of(0, 0, 1), ft)
     peers = [(lax.rem(dp + k, DP), ft) for k in range(1, DP)]
+    places = [(2, 1), (1, 1), (-1, 1), (2, 0), (0, 1), (1, 0), (-1, 0)]
+    members = [(place, (dp, feat_of(*place))) for place in places]
 
     waiting = []
     counts = [0, 0, 0]
@@ -73,8 +77,8 @@
         return math.prod(ref.shape) * jnp.dtype(ref.dtype).itemsize
 
     def all_of(sem, total):
-        count = total // (16 * 2 * WIDE)
-        ref = wout.at[pl.ds(0, 16 * count)]
+        assert total % (16 * WIDE) == 0
+        ref = wout.at[pl.ds(0, total // WIDE), pl.ds(0, WIDE // 2)]
         return pltpu.make_async_copy(ref, ref, sem)
 
     class Sender:
@@ -127,11 +131,14 @@
         return copy
 
     in_emb = [fetch(emb_a, emb.at[pl.ds(0, ROWS)]), fetch(emb_b, emb.at[pl.ds(ROWS, ROWS)])]
-    in_win = fetch(w_in, win)
+    in_win = [
+        fetch(w_in.at[:, pl.ds(k * TILE, TILE)], win.at[:, pl.ds(k * TILE, TILE)])
+        for k in range(WIDE // TILE)
+    ]
     in_gs = [fetch(gain, gn_sh.at[pl.ds(0, 1)]), fetch(shift, gn_sh.at[pl.ds(1, 1)])]
 
     barrier = pltpu.get_barrier_semaphore()
-    greeted = peers + [x_right, x_left, y_pair]
+    greeted = peers + [member for _, member in members]
     for device in greeted:
         pl.semaphore_signal(barrier, inc=1, device_id=device, device_id_type=MESH)
 
@@ -152,32 +159,29 @@
         )
         return center, lax.rsqrt(spread / BATCH + epsilon)
 
-    def first_layer():
-        for copy in in_emb:
-            copy.wait()
-        in_win.wait()
-        waiting.append(fetch(w_out, wout))
-
-        def tile(cols):
-            product = jnp.dot(emb[...], win[:, cols], preferred_element_type=f32)
-            for v in range(2):
-                piece = product[v * ROWS : (v + 1) * ROWS]
-                hid[v, :, cols] = piece
-                local_moments(piece, st1, 2 * v, cols)
-
-        column_tiles(tile)
-        pl.semaphore_wait(barrier, len(greeted))
+    def first_layer(v):
+        in_emb[v].wait()
+        for k, copy in enumerate(in_win):
+            cols = pl.ds(k * TILE, TILE)
+            if v == 0:
+                copy.wait()
+            hid[v, :, cols] = jnp.dot(emb[rows(v), :], win[:, cols], preferred_element_type=f32)
+            local_moments(hid[v, :, cols], st1.at[v], 0, cols)
 
     def first_norm(v):
+        first_layer(v)
         if v == 0:
-            exchange = Share(st1)
-            yield
-            exchange.wait_recv()
+            waiting.append(fetch(w_out, wout))
+            pl.semaphore_wait(barrier, len(greeted))
+        exchange = Share(st1.at[v])
+        yield
+        exchange.wait_recv()
+        if v == 0:
             for copy in in_gs:
                 copy.wait()
 
         def tile(cols):
-            center, inverse = global_moments(st1, 2 * v, cols)
+            center, inverse = global_moments(st1.at[v], 0, cols)
             hat = (hid[v, :, cols] - center) * inverse
             hid[v, :, cols] = hat
             inv[v : v + 1, cols] = inverse
@@ -185,7 +189,6 @@
             act[v, ft, :, cols] = jnp.maximum(before, 0.0).astype(bf16)
 
         column_tiles(tile)
-        yield
 
     def project(v, slot, first=False):
         def tile(cols):
@@ -235,7 +238,9 @@
         g = go_(slot(1, 0), left, high)
         if split:
             late.append(go_(slot(1, 0), pair, middle))
+        yield
         have(-1, 0)
+        yield
         have(1, 0)
         yield
         arrive(d[0])
@@ -243,7 +248,9 @@
         arrive(e[0])
         i = go_(slot(1, 1), left, bottom)
         arrive(*d[1:], *e[1:], *late)
+        yield
         have(-1, 1)
+        yield
         have(1, 1)
         yield
         arrive(f, g)
@@ -307,76 +314,26 @@
 
     def sum_gram(v):
         send = Sender()
-        low, high = pl.ds(0, BATCH // 2), pl.ds(BATCH // 2, BATCH // 2)
-
-        def pair_rows(step):
-            return pl.ds(pl.multiple_of(at_x(step) * 32, 32), 32)
-
-        far_right = send(part.at[v, pair_rows(2), low], far_g.at[v, 0], x_right)
-        far_left = send(part.at[v, pair_rows(2), high], far_g.at[v, 1], x_left)
-        near_gs[v, 0] = part[v, pair_rows(1), :]
-        near_gs[v, 1] = part[v, pair_rows(-1), :]
-        near = [
-            send(near_gs.at[v, 0, :, high], near_gr.at[v, 0, :, high], x_right),
-            send(near_gs.at[v, 1, :, low], near_gr.at[v, 1, :, low], x_left),
+
+        def block(step, flip):
+            return pl.ds(pl.multiple_of(feat_of(step, flip) * 16, 16), 16)
+
+        mine = block(0, 0)
+        arrivals = [
+            send(part.at[v, block(*place)], sum_r.at[v, n], member)
+            for n, (place, member) in enumerate(members)
         ]
         yield
-        far_right.wait_recv()
-        near_gs[v, 0, :, low] = (
-            near_gs[v, 0, :, low].astype(f32) + far_g[v, 0].astype(f32)
-        ).astype(bf16)
-        near.append(send(near_gs.at[v, 0, :, low], near_gr.at[v, 0, :, low], x_right))
-        far_left.wait_recv()
-        near_gs[v, 1, :, high] = (
-            near_gs[v, 1, :, high].astype(f32) + far_g[v, 1].astype(f32)
-        ).astype(bf16)
-        near.append(send(near_gs.at[v, 1, :, high], near_gr.at[v, 1, :, high], x_left))
-        yield
-        for copy in near:
+        total = part[v, mine, :].astype(f32)
+        for n, copy in enumerate(arrivals):
             copy.wait_recv()
-
-        def line_sum(flip):
-            h = y_hi + flip * (1 - 2 * y_hi)
-            block = pl.ds(pl.multiple_of(h * 16, 16), 16)
-            return (
-                part[v, pl.ds(pl.multiple_of(feat_of(0, flip) * 16, 16), 16), :].astype(f32)
-                + near_gr[v, 0, block, :].astype(f32)
-                + near_gr[v, 1, block, :].astype(f32)
-            )
-
-        y_gs[v] = line_sum(1).astype(bf16)
-        a = send(y_gs.at[v], y_gr.at[v], y_pair)
-        yield
-        a.wait_recv()
-
-        def slot(step, flip=0):
-            return pl.ds(pl.multiple_of(feat_of(step, flip) * 16, 16), 16)
-
-        gram[v, slot(0), :] = (line_sum(0) + y_gr[v].astype(f32)).astype(bf16)
-
-        def go_(block, device, cols=None):
-            ref = gram.at[v, block] if cols is None else gram.at[v, block, cols]
-            return send(ref, ref, device)
-
-        a = go_(slot(0), y_pair)
-        b = go_(slot(0), x_right)
-        c = go_(slot(0), x_left)
-        yield
-        a.wait_recv()
-        d = go_(slot(0, 1), x_right)
-        e = go_(slot(0, 1), x_left)
-        yield
-        b.wait_recv()
-        f = go_(slot(-1), x_right, low)
-        c.wait_recv()
-        g = go_(slot(1), x_left, high)
-        yield
-        d.wait_recv()
-        h = go_(slot(-1, 1), x_right, low)
-        e.wait_recv()
-        i = go_(slot(1, 1), x_left, high)
-        yield
-        for copy in (f, g, h, i):
+            total += sum_r[v, n].astype(f32)
+        gram[v, mine, :] = total.astype(bf16)
+        arrivals = [
+            send(gram.at[v, mine], gram.at[v, mine], member) for _, member in members
+        ]
+        yield
+        for copy in arrivals:
             copy.wait_recv()
 
     factor = BATCH / 64.0
@@ -432,7 +389,7 @@
     def active_back(v, h):
         send = Sender()
         def block(step, flip, store):
-            first = feat_of(step, flip) * WIDE + h * PIECE
+            first = feat_of(step, flip) * WIDE + STARTS[h]
 
             def tile(cols):
                 store(
@@ -443,17 +400,17 @@
                     ),
                 )
 
-            column_tiles(tile, PIECE)
+            column_tiles(tile, PIECES[h])
 
         edge = BACK_EDGE[v][h]
         top, bottom = pl.ds(0, edge), pl.ds(ROWS - edge, edge)
         middle, between = pl.ds(edge, ROWS - 2 * edge), pl.ds(0, ROWS - 2 * edge)
-        mine = pl.ds(h * PIECE, PIECE)
+        mine, here = pl.ds(STARTS[h], PIECES[h]), pl.ds(0, PIECES[h])
         crossed = {}
 
         def cross(step, ref):
             slot = (2, 1, -1, 0).index(step)
-            crossed[step] = send(ref, cross_r.at[v, h, slot, between], y_pair)
+            crossed[step] = send(ref, cross_r.at[v, h, slot, between, here], y_pair)
 
         def added(step, ref):
             slot = (2, 1, -1, 0).index(step)
@@ -468,15 +425,15 @@
             return store
 
         def far(flip):
-            ref = far_s.at[v, h, flip]
+            ref = far_s.at[v, h, flip, :, here]
             block(2, flip, keep(ref) if flip else added(2, ref))
             if flip:
                 cross(2, ref.at[middle])
             first, second = (top, bottom) if flip else (low, high)
             into = between_half if not flip else pl.ds(0, edge)
             return [
-                send(ref.at[first], far_r.at[v, h, flip, 0, into], x_right),
-                send(ref.at[second], far_r.at[v, h, flip, 1, into], x_left),
+                send(ref.at[first], far_r.at[v, h, flip, 0, into, here], x_right),
+                send(ref.at[second], far_r.at[v, h, flip, 1, into, here], x_left),
             ]
 
         low, high = pl.ds(0, HALF), pl.ds(HALF, HALF)
@@ -486,10 +443,10 @@
             first, second = (top, bottom) if flip else (low, high)
             copies = []
             for side, step, part_rows, device in ((0, 1, second, x_right), (1, -1, first, x_left)):
-                ref = near_s.at[v, h, flip, side]
+                ref = near_s.at[v, h, flip, side, :, here]
                 block(step, flip, keep(ref) if flip else added(step, ref))
                 copies.append(
-                    send(ref.at[part_rows], near_r.at[v, h, flip, side, part_rows], device)
+                    send(ref.at[part_rows], near_r.at[v, h, flip, side, part_rows, here], device)
                 )
                 if flip:
                     cross(step, ref.at[middle])
@@ -500,19 +457,19 @@
             into = between_half if not flip else pl.ds(0, edge)
             for side, part_rows, device in ((0, first, x_right), (1, second, x_left)):
                 fars[side].wait_recv()
-                near_s[v, h, flip, side, part_rows] = (
-                    near_s[v, h, flip, side, part_rows].astype(f32)
-                    + far_r[v, h, flip, side, into].astype(f32)
+                near_s[v, h, flip, side, part_rows, here] = (
+                    near_s[v, h, flip, side, part_rows, here].astype(f32)
+                    + far_r[v, h, flip, side, into, here].astype(f32)
                 ).astype(bf16)
                 nears.append(
                     send(
-                        near_s.at[v, h, flip, side, part_rows],
-                        near_r.at[v, h, flip, side, part_rows], device,
+                        near_s.at[v, h, flip, side, part_rows, here],
+                        near_r.at[v, h, flip, side, part_rows, here], device,
                     )
                 )
 
         def store_own(cols, value):
-            gact[v, :, pl.ds(pl.multiple_of(h * PIECE + cols.start, TILE), TILE)] = value
+            gact[v, :, pl.ds(pl.multiple_of(STARTS[h] + cols.start, TILE), TILE)] = value
 
         def store_pair(cols, value):
             store_own(cols, value)
@@ -523,7 +480,7 @@
         nears1 = near(1)
         yield
         block(0, 1, store_pair)
-        cross(0, cross_s.at[v, h, between])
+        cross(0, cross_s.at[v, h, between, here])
         yield
         fars0 = far(0)
         yield
@@ -534,13 +491,13 @@
         for copy in nears1:
             copy.wait_recv()
         for place, part_rows in ((pl.ds(0, edge), top), (pl.ds(edge, edge), bottom)):
-            ys[v, h, place] = (
+            ys[v, h, place, here] = (
                 gact[v, part_rows, mine]
-                + near_r[v, h, 1, 0, part_rows].astype(f32)
-                + near_r[v, h, 1, 1, part_rows].astype(f32)
+                + near_r[v, h, 1, 0, part_rows, here].astype(f32)
+                + near_r[v, h, 1, 1, part_rows, here].astype(f32)
             ).astype(bf16)
         edges = pl.ds(0, 2 * edge)
-        last = send(ys.at[v, h, edges], yr.at[v, h, edges], y_pair)
+        last = send(ys.at[v, h, edges, here], yr.at[v, h, edges, here], y_pair)
         yield
         block(0, 0, store_own)
         yield
@@ -552,7 +509,7 @@
     def first_back(h):
         def tile(v, cols):
             edge = BACK_EDGE[v][h]
-            full = pl.ds(pl.multiple_of(h * PIECE + cols.start, TILE), TILE)
+            full = pl.ds(pl.multiple_of(STARTS[h] + cols.start, TILE), TILE)
             hat = hid[v, :, full]
             grad = (
                 gact[v, :, full]
@@ -572,15 +529,15 @@
             st4[h, dp, 2 * v : 2 * v + 1, cols] = jnp.sum(grad, axis=0, keepdims=True)
             st4[h, dp, 2 * v + 1 : 2 * v + 2, cols] = jnp.sum(grad * hat, axis=0, keepdims=True)
 
-        column_tiles(functools.partial(tile, 1), PIECE)
-        yield
-        column_tiles(functools.partial(tile, 0), PIECE)
-        exchange = Share(st4.at[h])
+        column_tiles(functools.partial(tile, 1), PIECES[h])
+        yield
+        column_tiles(functools.partial(tile, 0), PIECES[h])
+        exchange = Share(st4.at[h, :, :, pl.ds(0, PIECES[h])])
         yield
         exchange.wait_recv()
 
         def finish(cols):
-            full = pl.ds(pl.multiple_of(h * PIECE + cols.start, TILE), TILE)
+            full = pl.ds(pl.multiple_of(STARTS[h] + cols.start, TILE), TILE)
             sums = [jnp.sum(st4[h, :, k, cols], axis=0, keepdims=True) for k in range(4)]
             for v in range(2):
                 up, dot = sums[2 * v], sums[2 * v + 1]
@@ -591,7 +548,7 @@
             grad_shift[:, full] = sums[0] + sums[2]
             grad_gain[:, full] = sums[1] + sums[3]
 
-        column_tiles(finish, PIECE)
+        column_tiles(finish, PIECES[h])
 
     def transpose_emb():
         for k in range(EMB // ROWS):
@@ -600,11 +557,11 @@
 
     def last_layer(h):
         send = Sender()
+        mine, here = pl.ds(STARTS[h], PIECES[h]), pl.ds(0, PIECES[h])
         low, high = pl.ds(0, OUT // 2), pl.ds(OUT // 2, OUT // 2)
-        mine = pl.ds(h * PIECE, PIECE)
 
         def product(cols):
-            full = pl.ds(pl.multiple_of(h * PIECE + cols.start, TILE), TILE)
+            full = pl.ds(pl.multiple_of(STARTS[h] + cols.start, TILE), TILE)
             win[:, full] = jnp.dot(
                 emb_t[...], gh[:, full], preferred_element_type=f32
             ).astype(bf16)
@@ -613,47 +570,47 @@
             target = dp_of(step, flip_y, flip_core)
             return win.at[pl.ds(pl.multiple_of(target * OUT, OUT), OUT), mine]
 
-        column_tiles(product, PIECE)
+        column_tiles(product, PIECES[h])
         order = [(2, 1), (1, 1), (-1, 1), (2, 0), (1, 0), (-1, 0), (0, 1), (0, 0)]
         crossing = {}
         for n, (step, flip) in enumerate(order):
-            crossing[step, flip] = send(block(step, flip, 1), core_r.at[h, n], other)
+            crossing[step, flip] = send(block(step, flip, 1), core_r.at[h, n, :, here], other)
         yield
 
         def chip_sum(step, flip):
             n = order.index((step, flip))
             crossing[step, flip].wait_recv()
-            return block(step, flip, 0)[...].astype(f32) + core_r[h, n].astype(f32)
+            return block(step, flip, 0)[...].astype(f32) + core_r[h, n, :, here].astype(f32)
 
         def far(flip):
-            far_is[h, flip] = chip_sum(2, flip).astype(bf16)
+            far_is[h, flip, :, here] = chip_sum(2, flip).astype(bf16)
             return [
-                send(far_is.at[h, flip, low], far_ir.at[h, flip, 0], z_right),
-                send(far_is.at[h, flip, high], far_ir.at[h, flip, 1], z_left),
+                send(far_is.at[h, flip, low, here], far_ir.at[h, flip, 0, :, here], z_right),
+                send(far_is.at[h, flip, high, here], far_ir.at[h, flip, 1, :, here], z_left),
             ]
 
         def near(flip):
-            near_is[h, flip, 0] = chip_sum(1, flip).astype(bf16)
-            a = send(near_is.at[h, flip, 0, high], near_ir.at[h, flip, 0, high], z_right)
-            near_is[h, flip, 1] = chip_sum(-1, flip).astype(bf16)
-            b = send(near_is.at[h, flip, 1, low], near_ir.at[h, flip, 1, low], z_left)
+            near_is[h, flip, 0, :, here] = chip_sum(1, flip).astype(bf16)
+            a = send(near_is.at[h, flip, 0, high, here], near_ir.at[h, flip, 0, high, here], z_right)
+            near_is[h, flip, 1, :, here] = chip_sum(-1, flip).astype(bf16)
+            b = send(near_is.at[h, flip, 1, low, here], near_ir.at[h, flip, 1, low, here], z_left)
             return [a, b]
 
         def relay(flip, fars, nears):
             for side, half, device in ((0, low, z_right), (1, high, z_left)):
                 fars[side].wait_recv()
-                near_is[h, flip, side, half] = (
-                    near_is[h, flip, side, half].astype(f32) + far_ir[h, flip, side].astype(f32)
+                near_is[h, flip, side, half, here] = (
+                    near_is[h, flip, side, half, here].astype(f32) + far_ir[h, flip, side, :, here].astype(f32)
                 ).astype(bf16)
                 nears.append(
-                    send(near_is.at[h, flip, side, half], near_ir.at[h, flip, side, half], device)
+                    send(near_is.at[h, flip, side, half, here], near_ir.at[h, flip, side, half, here], device)
                 )
 
         def line_sum(flip):
             return (
                 chip_sum(0, flip)
-                + near_ir[h, flip, 0].astype(f32)
-                + near_ir[h, flip, 1].astype(f32)
+                + near_ir[h, flip, 0, :, here].astype(f32)
+                + near_ir[h, flip, 1, :, here].astype(f32)
             )
 
         fars1 = far(1)
@@ -667,14 +624,15 @@
         yield
         for copy in nears1:
             copy.wait_recv()
-        y_is[h] = line_sum(1).astype(bf16)
-        last = send(y_is.at[h], y_ir.at[h], y_next)
+        y_is[h, :, here] = line_sum(1).astype(bf16)
+        last = send(y_is.at[h, :, here], y_ir.at[h, :, here], y_next)
         yield
         relay(0, fars0, nears0)
         yield
         for copy in nears0 + [last]:
             copy.wait_recv()
-        gout[:, mine] = line_sum(0) + y_ir[h].astype(f32)
+        total = line_sum(0)
+        gout[:, mine] = total + y_ir[h, :, here].astype(f32)
         stores.append(fetch(gout.at[:, mine], grad_in.at[:, mine]))
 
     def once(stage, *args):
@@ -693,18 +651,18 @@
     loss, row = once(losses), once(row_losses)
     turn = once(transpose_emb)
     order = (
-        first_a, first_a, feat_a, feat_a, first_b, feat_a, feat_a, feat_b, feat_a, turn, feat_a,
-        norm_a, feat_b, norm_a, dp_a, feat_b, feat_b, dp_a, dp_a, feat_b, feat_b, norm_b, dp_a,
-        dp_a, norm_b, dp_b, dp_a, gram_a, gram_a, dp_b, gram_a, dp_b, gram_a, dp_b, gram_a, dp_b,
-        dp_b, gram_b, gram_a, gram_b, loss, gram_a, gram_b, gram_a, back_b, gram_b, back_b, act_b1,
-        gram_b, act_b0, act_b0, act_b1, gram_b, act_b0, act_b1, gram_b, act_b1, act_b1, act_b0,
-        act_b0, act_b0, act_b1, gram_b, back_a, act_b1, act_b1, act_b1, act_b0, act_b0, act_b0,
-        back_a, act_a1, act_a0, act_a1, act_a0, act_b1, act_a0, act_a1, act_a1, act_a1, act_a0,
-        act_a0, act_b0, row, act_a1, pre_1, act_a1, act_a1, act_a1, act_a0, act_a0, act_a0, act_a0,
-        act_a1, pre_1, pre_0, act_a0, pre_0, pre_1, last_1, pre_0, last_1, last_0, last_1, last_0,
-        last_1, last_0, last_0, last_1, last_0, last_1, last_1, last_0, last_0, last_1, last_0,
+        first_a, first_a, feat_a, feat_a, feat_a, feat_a, first_b, feat_a, first_b, feat_a, feat_b,
+        feat_a, feat_a, feat_a, feat_a, norm_a, feat_b, norm_a, dp_a, feat_b, feat_b, feat_b,
+        feat_b, feat_b, dp_a, feat_b, feat_b, feat_b, norm_b, dp_a, dp_a, dp_a, dp_a, dp_a, norm_b,
+        dp_a, dp_b, dp_a, dp_a, gram_a, dp_b, dp_b, dp_b, dp_b, dp_b, gram_a, dp_b, dp_b, dp_b,
+        dp_b, gram_b, gram_a, turn, loss, back_b, gram_b, back_b, act_b0, act_b0, act_b1, act_b0,
+        act_b1, act_b1, gram_b, back_a, act_b0, act_b0, act_b1, act_b0, back_a, act_a1, act_a0,
+        act_a1, act_b1, act_a1, act_a1, act_a1, act_a0, act_a1, act_b1, act_a0, act_a0, act_b1,
+        act_a1, act_b1, act_a0, act_a1, act_b1, act_b0, act_b0, act_a1, act_a0, act_b0, act_a0,
+        act_b1, act_a0, act_a0, act_a1, pre_1, pre_1, act_b0, pre_0, act_a0, pre_0, pre_1, last_1,
+        pre_0, last_1, last_0, last_1, last_0, last_1, last_0, last_0, last_1, last_0, last_1,
+        last_1, last_0, last_0, row, last_1, last_0,
     )
-    first_layer()
     for stage in order:
         next(stage, None)
     for stage in order:
@@ -727,12 +685,11 @@
         v((2 * ROWS, EMB), bf16), v((EMB, WIDE), bf16), v((FEAT * WIDE, WIDE), bf16),
         v((2, WIDE), f32), v((4, WIDE), f32), v((2, ROWS, WIDE), f32), v((2, FEAT, ROWS, WIDE), bf16),
         v((2, ROWS, WIDE), f32),
-        v((DP, 4, WIDE), f32), v((2, DP, 2, WIDE), f32),
+        v((2, DP, 2, WIDE), f32), v((2, DP, 2, WIDE), f32),
         v((2, DP, 2, WIDE), f32), v((2, DP, 4, PIECE), f32),
         v((2, DP, ROWS, WIDE), bf16), v((DP, WIDE), f32),
-        v((2, ROWS, BATCH), bf16), v((2, 2, 32, BATCH // 2), bf16),
-        v((2, 2, 32, BATCH), bf16), v((2, 2, 32, BATCH), bf16),
-        v((2, 16, BATCH), bf16), v((2, 16, BATCH), bf16), v((2, ROWS, BATCH), bf16),
+        v((2, ROWS, BATCH), bf16), v((2, FEAT - 1, 16, BATCH), bf16),
+        v((2, ROWS, BATCH), bf16),
         v((2, ROWS, WIDE), bf16),
         v((2, 2, 2, ROWS, PIECE), bf16), v((2, 2, 2, 2, HALF, PIECE), bf16),
         v((2, 2, 2, 2, ROWS, PIECE), bf16), v((2, 2, 2, 2, ROWS, PIECE), bf16),
@@ -743,8 +700,8 @@
         v((2, 2, OUT, PIECE), bf16), v((2, 2, 2, OUT // 2, PIECE), bf16),
         v((2, 2, 2, OUT, PIECE), bf16), v((2, 2, 2, OUT, PIECE), bf16),
         v((2, OUT, PIECE), bf16), v((2, OUT, PIECE), bf16), v((OUT, WIDE), f32),
-        pltpu.SemaphoreType.DMA((21,)), pltpu.SemaphoreType.DMA((216,)),
-        pltpu.SemaphoreType.DMA((8,)),
+        pltpu.SemaphoreType.DMA((22,)), pltpu.SemaphoreType.DMA((198,)),
+        pltpu.SemaphoreType.DMA((11,)),
     ]
 
 

time: 163 us -> 158 us (0.969)
  Pallas kernels: 162 us -> 157 us
    pallas_call x1, Pallas kernels: 160 us -> 155 us  [shards(): pl.pallas_call(kernel, out_shape=(jax.ShapeDtypeStruct((OUT, WIDE), f32),...]
where the time goes in v4:
time: 158 us
  Pallas kernels  157 us (99%)
    pallas_call x1, Pallas kernels, shards(): pl.pallas_call(kernel, out_shape=(jax.ShapeDtypeStruct((OUT, WIDE), f32),...  155 us

profile of v4, /device:TPU:0, one launch (start us, length us, event | category | flops | bytes accessed | tf_op | source)
XLA Modules:
  0.0 157.8 jit_solution(6581628493223879255)
XLA Ops:
  0.6 155.4 %shard_map.101 = (f32[96,1024]{1,0:T(8,128)}, f32[1,1024]{1,0:T(1,128)}, f32[1,1024]{1,0:T(1,128)}, f32[1,1024]{1,0:T(1,128)}, f32[1,128]{1,0:T(1,128)}) custom-call(bf16[128,1536]{1,0:T(8,128)(2,1)} %emb_a.1, bf16[128,1536]{1,0:T(8,128)(2,1)} %emb_b.1, bf16[1536,1024]{1,0:T(8,128)(2,1)} %w_in.1, bf16[8192,1024]{1,0:T(8,128)(2,1)} %w_out.1, ...), custom_call_target="tpu_custom_call" | custom-call | flops 14000000000 | bytes 25165824 | tf_op jit(solution)/shard_map/pallas_call | solution.py:711
  156.0 1.8 %shard_map.102 = (f32[96,1024]{1,0:T(8,128)}, f32[1,1024]{1,0:T(1,128)}, f32[1,1024]{1,0:T(1,128)}, f32[1,1024]{1,0:T(1,128)}, f32[1,128]{1,0:T(1,128)}) custom-call(f32[96,1024]{1,0:T(8,128)} %get-tuple-element.15.refs_0_, f32[1,1024]{1,0:T(1,128)} %get-tuple-element.16.refs_1_, f32[1,1024]{1,0:T(1,128)} %get-tuple-element.17.refs_2_, ...), custom_call_target="tpu_custom_call" | custom-call | tf_op jit(solution)/shard_map/pallas_call | solution.py:728

commit v5 on v4

--- a/solution.py
+++ b/solution.py
@@ -651,17 +651,17 @@
     loss, row = once(losses), once(row_losses)
     turn = once(transpose_emb)
     order = (
-        first_a, first_a, feat_a, feat_a, feat_a, feat_a, first_b, feat_a, first_b, feat_a, feat_b,
-        feat_a, feat_a, feat_a, feat_a, norm_a, feat_b, norm_a, dp_a, feat_b, feat_b, feat_b,
+        first_a, first_a, feat_a, feat_a, first_b, feat_a, feat_a, first_b, feat_a, feat_a, feat_a,
+        feat_b, feat_a, feat_a, feat_a, norm_a, feat_b, norm_a, dp_a, feat_b, feat_b, feat_b, turn,
         feat_b, feat_b, dp_a, feat_b, feat_b, feat_b, norm_b, dp_a, dp_a, dp_a, dp_a, dp_a, norm_b,
-        dp_a, dp_b, dp_a, dp_a, gram_a, dp_b, dp_b, dp_b, dp_b, dp_b, gram_a, dp_b, dp_b, dp_b,
-        dp_b, gram_b, gram_a, turn, loss, back_b, gram_b, back_b, act_b0, act_b0, act_b1, act_b0,
-        act_b1, act_b1, gram_b, back_a, act_b0, act_b0, act_b1, act_b0, back_a, act_a1, act_a0,
-        act_a1, act_b1, act_a1, act_a1, act_a1, act_a0, act_a1, act_b1, act_a0, act_a0, act_b1,
-        act_a1, act_b1, act_a0, act_a1, act_b1, act_b0, act_b0, act_a1, act_a0, act_b0, act_a0,
-        act_b1, act_a0, act_a0, act_a1, pre_1, pre_1, act_b0, pre_0, act_a0, pre_0, pre_1, last_1,
-        pre_0, last_1, last_0, last_1, last_0, last_1, last_0, last_0, last_1, last_0, last_1,
-        last_1, last_0, last_0, row, last_1, last_0,
+        dp_b, dp_a, dp_a, dp_a, gram_a, dp_b, dp_b, dp_b, dp_b, dp_b, dp_b, gram_a, dp_b, dp_b,
+        dp_b, gram_b, gram_a, loss, back_b, gram_b, back_b, act_b1, act_b1, act_b1, act_b0, act_b0,
+        act_b0, gram_b, act_b1, back_a, act_b0, act_b0, act_b0, back_a, act_a1, act_b1, act_a0,
+        act_a0, act_a0, act_a1, act_a1, act_b0, act_a1, act_b0, act_a0, act_a0, act_b0, act_b1,
+        act_b1, act_a1, act_b1, act_a0, act_b0, act_a0, act_a0, act_a0, act_a1, act_a1, act_a1,
+        act_b1, act_a1, act_a0, pre_0, pre_0, act_b1, pre_1, act_a1, pre_1, pre_0, last_0, pre_1,
+        last_0, last_1, last_0, last_1, last_0, last_1, last_1, last_0, last_1, last_0, last_0,
+        last_1, last_1, row, last_0, last_1,
     )
     for stage in order:
         next(stage, None)

time: 158 us -> 156 us (0.987)
  Pallas kernels: 157 us -> 155 us
    pallas_call x1, Pallas kernels: 155 us -> 153 us  [shards(): pl.pallas_call(kernel, out_shape=(jax.ShapeDtypeStruct((OUT, WIDE), f32),...]
where the time goes in v5:
time: 156 us; the launch traced here: 155 us
  Pallas kernels  155 us (99%)
    pallas_call x1, Pallas kernels, shards(): pl.pallas_call(kernel, out_shape=(jax.ShapeDtypeStruct((OUT, WIDE), f32),...  153 us

profile of v5, /device:TPU:0, one launch (start us, length us, event | category | flops | bytes accessed | tf_op | source)
XLA Modules:
  0.0 155.4 jit_solution(10641867354619144733)
XLA Ops:
  0.6 152.9 %shard_map.101 = (f32[96,1024]{1,0:T(8,128)}, f32[1,1024]{1,0:T(1,128)}, f32[1,1024]{1,0:T(1,128)}, f32[1,1024]{1,0:T(1,128)}, f32[1,128]{1,0:T(1,128)}) custom-call(bf16[128,1536]{1,0:T(8,128)(2,1)} %emb_a.1, bf16[128,1536]{1,0:T(8,128)(2,1)} %emb_b.1, bf16[1536,1024]{1,0:T(8,128)(2,1)} %w_in.1, bf16[8192,1024]{1,0:T(8,128)(2,1)} %w_out.1, ...), custom_call_target="tpu_custom_call" | custom-call | flops 14000000000 | bytes 25165824 | tf_op jit(solution)/shard_map/pallas_call | solution.py:711
  153.6 1.8 %shard_map.102 = (f32[96,1024]{1,0:T(8,128)}, f32[1,1024]{1,0:T(1,128)}, f32[1,1024]{1,0:T(1,128)}, f32[1,1024]{1,0:T(1,128)}, f32[1,128]{1,0:T(1,128)}) custom-call(f32[96,1024]{1,0:T(8,128)} %get-tuple-element.15.refs_0_, f32[1,1024]{1,0:T(1,128)} %get-tuple-element.16.refs_1_, f32[1,1024]{1,0:T(1,128)} %get-tuple-element.17.refs_2_, ...), custom_call_target="tpu_custom_call" | custom-call | tf_op jit(solution)/shard_map/pallas_call | solution.py:728
